TPU v7x, 32 devices: a whole 2x2x4 slice. The times are simulated.
32 devices in a mesh: section: 2 (over core), dp: 8 (over z, x), rep: 2 (over y).
Axes of the slice: x: 2, y: 2, z: 4, core: 2. Of those that a mesh axis runs over, the one named last changes fastest.
Arguments:
- query_crops: bfloat16 [32, 256, 768], P(('dp', 'rep'), 'section'), may hold values from -5 to 5
- key_crops: bfloat16 [32, 256, 768], P(('dp', 'rep'), 'section'), may hold values from -5 to 5
- query_lengths: int32 [32], P(('dp', 'rep')), may hold values from 64 to 256, as said below
- key_lengths: int32 [32], P(('dp', 'rep')), may hold values from 64 to 256, as said below
- positive: int32 [32], P(('dp', 'rep')), may hold values from 0 to 31, as said below
- queue: bfloat16 [4096, 768], replicated, may hold values from -6 to 6
- qkv_weight: bfloat16 [2, 768, 2304], P('section'), may hold values from -0.21875 to 0.21875
- out_weight: bfloat16 [2, 768, 768], P('section'), may hold values from -0.875 to 0.875
- up_weight: bfloat16 [2, 768, 3072], P('section'), may hold values from -0.21875 to 0.21875
- down_weight: bfloat16 [2, 3072, 768], P('section'), may hold values from -0.109375 to 0.109375
- biases: bfloat16 [2, 5, 768], P('section'), may hold values from -1.25 to 1.25
- gains: bfloat16 [2, 2, 768], P('section'), may hold values from 0.5 to 1.5
- up_biases: bfloat16 [2, 3072], P('section'), may hold values from -1.25 to 1.25
- query_bias: bfloat16 [2, 768], P('section'), may hold values from -1.25 to 1.25
- key_qkv_weight: bfloat16 [2, 768, 2304], P('section'), may hold values from -0.21875 to 0.21875
- key_out_weight: bfloat16 [2, 768, 768], P('section'), may hold values from -0.875 to 0.875
- key_up_weight: bfloat16 [2, 768, 3072], P('section'), may hold values from -0.21875 to 0.21875
- key_down_weight: bfloat16 [2, 3072, 768], P('section'), may hold values from -0.109375 to 0.109375
- key_biases: bfloat16 [2, 6, 768], P('section'), may hold values from -1.25 to 1.25
- key_gains: bfloat16 [2, 2, 768], P('section'), may hold values from 0.5 to 1.5
- key_up_biases: bfloat16 [2, 3072], P('section'), may hold values from -1.25 to 1.25
Outputs:
- loss: float32 [1], replicated
- crops_grad: float32 [32, 256, 768], P(('dp', 'rep'), 'section')
- qkv_weight_grad: float32 [2, 768, 2304], P('section', ('dp', 'rep'))
- out_weight_grad: float32 [2, 768, 768], P('section', ('dp', 'rep'))
- up_weight_grad: float32 [2, 768, 3072], P('section', ('dp', 'rep'))
- down_weight_grad: float32 [2, 3072, 768], P('section', ('dp', 'rep'))
- biases_grad: float32 [2, 5, 768], P('section', None, ('dp', 'rep'))
- gains_grad: float32 [2, 2, 768], P('section', None, ('dp', 'rep'))
- up_biases_grad: float32 [2, 3072], P('section', ('dp', 'rep'))
- query_bias_grad: float32 [2, 768], P('section', ('dp', 'rep'))
Inputs may be any that keep to these rules, and one draw needn't show every extreme that they name: `query_lengths`: some crop has exactly 256 real tokens and some exactly 64. `key_lengths`: some crop has exactly 256 real tokens and some exactly 64. A permutation: every key crop is the positive of exactly one query crop.
All inputs are finite; a program needn't handle non-finite values.
Results may differ from a plain program's by a relative error of at most 0.0095.
Values may be sent and summed in bfloat16 or wider, within the bound.
No kernel may reach another device: no remote copies, remote signals or barrier semaphores. Data moves between devices by JAX's collectives and lax.ppermute only.
A program may use at most 192 MiB of HBM per device.

v0:
```python
import functools

import jax
import jax.numpy as jnp
from jax import lax
from jax.experimental import pallas as pl
from jax.experimental.pallas import tpu as pltpu
from jax.sharding import PartitionSpec as P

F32 = jnp.float32
BF = jnp.bfloat16
MASKED = -1e30
D = 768
FF = 3072
SLOTS = 256
PAIRS = 6
MIB = 2**20
SEMS = 96


def dot(a, b):
    return lax.dot_general(a, b, (((1,), (0,)), ((), ())), preferred_element_type=F32)


def dot_nt(a, b):
    return lax.dot_general(a, b, (((1,), (1,)), ((), ())), preferred_element_type=F32)


def dot_tn(a, b):
    return lax.dot_general(a, b, (((0,), (0,)), ((), ())), preferred_element_type=F32)


def gelu_parts(x, want_slope):
    ax = jnp.abs(x)
    t = pl.reciprocal(1.0 + (0.3275911 * 0.7071067811865476) * ax)
    e = jnp.exp(-0.5 * (x * x))
    poly = (0.5 * 1.061405429) * t + 0.5 * -1.453152027
    poly = poly * t + 0.5 * 1.421413741
    poly = poly * t + 0.5 * -0.284496736
    poly = poly * t + 0.5 * 0.254829592
    q = poly * t * e
    g = jnp.maximum(x, 0.0) - ax * q
    if not want_slope:
        return g, None
    return g, jnp.where(x >= 0, 1.0 - q, q) + (0.3989422804014327 * x) * e


def norm_parts(z):
    mean = jnp.mean(z, axis=-1, keepdims=True)
    c = z - mean
    var = jnp.mean(c * c, axis=-1, keepdims=True)
    r = lax.rsqrt(var + 1e-12)
    return c * r, r


def head_masks(scale):
    lane = lax.broadcasted_iota(jnp.int32, (1, 128), 1)
    low = jnp.where(lane < 64, scale, 0.0).astype(BF)
    high = jnp.where(lane < 64, 0.0, scale).astype(BF)
    return low, high


def stack_heads(pair, scale):
    low, high = head_masks(scale)
    return jnp.concatenate([pair * low, pair * high], axis=0)


def side_by_side(stacked):
    half = stacked.shape[0] // 2
    return jnp.concatenate([stacked[:half], stacked[half:]], axis=1)


class Copies:
    def __init__(self, sems):
        self.sems, self.used, self.open = sems, 0, []

    def make(self, src, dst):
        self.used += 1
        return pltpu.make_async_copy(src, dst, self.sems.at[self.used - 1])

    def fetch(self, src, dst):
        cp = self.make(src, dst)
        cp.start()
        return cp

    def pick(self, by_section, dst):
        if by_section[0] is by_section[1]:
            return self.fetch(by_section[0], dst)
        sem = self.sems.at[self.used]
        self.used += 1
        here = lax.axis_index("section")

        @pl.when(here == 0)
        def _():
            pltpu.make_async_copy(by_section[0], dst, sem).start()

        @pl.when(here != 0)
        def _():
            pltpu.make_async_copy(by_section[1], dst, sem).start()

        return pltpu.make_async_copy(by_section[0], dst, sem)

    def send(self, src, dst):
        self.open.append(self.fetch(src, dst))

    def drain(self):
        for cp in self.open:
            cp.wait()


def only_on(section, run):
    if section is None:
        run()
    else:
        pl.when(lax.axis_index("section") == section)(run)


VMEM = pl.BlockSpec(memory_space=pltpu.VMEM)
ANY = pl.BlockSpec(memory_space=pl.ANY)
SMEM = pl.BlockSpec(memory_space=pltpu.SMEM)
sd = jax.ShapeDtypeStruct


def call(kernel, name, outs, out_specs, ins, in_specs, scratch, flops, moved):
    return pl.pallas_call(
        kernel,
        out_shape=[sd(*o) for o in outs],
        in_specs=in_specs,
        out_specs=out_specs,
        scratch_shapes=[pltpu.VMEM(*s) for s in scratch] + [pltpu.SemaphoreType.DMA((SEMS,))],
        compiler_params=pltpu.CompilerParams(vmem_limit_bytes=56 * MIB),
        cost_estimate=pl.CostEstimate(flops=flops, bytes_accessed=moved, transcendentals=0),
        name=name,
    )(*ins)


def saved_shapes(rows):
    crops = rows // SLOTS
    return [
        ((rows, 3 * D), BF),
        ((PAIRS * crops, 2 * SLOTS, SLOTS), BF),
        ((rows, D), BF),
        ((rows, D), BF),
        ((rows, 128), F32),
        ((rows, D), BF),
        ((rows, FF), BF),
        ((rows, FF), BF),
        ((rows, D), BF),
        ((rows, 128), F32),
    ]


def fetch_rows(copies, refs, kinds, x):
    waits = []
    half = refs[0].shape[1] if "halves" in kinds else SLOTS // 2
    for c in range(x.shape[0] // SLOTS):
        for h in range(SLOTS // half):
            at = slice(SLOTS * c + half * h, SLOTS * c + half * (h + 1))
            options = []
            if "halves" in kinds:
                options.append(refs[h].at[c])
            if "whole" in kinds:
                options.append(refs[-1].at[at, :])
            waits.append(copies.pick((options[0], options[-1]), x.at[at, :]))
    return waits


def read_vectors(refs, key):
    if key:
        b, g, up = refs
        rows = b[0].astype(F32)
        rows = [rows[i : i + 1] for i in range(6)]
    else:
        b, g, up, q = refs
        rows = b[0].astype(F32)
        rows = [q[...].astype(F32)] + [rows[i : i + 1] for i in range(5)]
    gains = g[0].astype(F32)
    return rows + [gains[0:1], gains[1:2]], up[...].astype(F32)


def load_vectors(refs, kinds, vec, bup):
    sets = []
    for kind in kinds:
        n = 3 if kind == "key" else 4
        sets.append(read_vectors(refs[:n], kind == "key"))
        refs = refs[n:]
    here = lax.axis_index("section")
    for i in range(8):
        row = sets[0][0][i]
        if len(sets) == 2:
            row = jnp.where(here == 0, row, sets[1][0][i])
        vec[i : i + 1, :] = row
    up = sets[0][1]
    if len(sets) == 2:
        up = jnp.where(here == 0, up, sets[1][1])
    bup[...] = up


def forward_kernel(rows, active, save, x_kinds, sets, *refs):
    def run():
        forward_body(rows, save, x_kinds, sets, *refs)

    only_on(active, run)


def forward_body(rows, save, x_kinds, sets, *refs):
    crops = rows // SLOTS
    lens_refs, refs = refs[: len(sets)], refs[len(sets) :]
    here = lax.axis_index("section")
    if len(sets) == 2:
        lens = [jnp.where(here == 0, lens_refs[0][c], lens_refs[1][c]) for c in range(crops)]
    else:
        lens = [lens_refs[0][c] for c in range(crops)]
    n_x = (2 if "halves" in x_kinds else 0) + (1 if "whole" in x_kinds else 0)
    x_refs, refs = refs[:n_x], refs[n_x:]
    w_refs, refs = refs[: 4 * len(sets)], refs[4 * len(sets) :]
    n_v = sum(3 if k == "key" else 4 for k in sets)
    v_refs, refs = refs[:n_v], refs[n_v:]
    y_ref, pool_ref = refs[:2]
    refs = refs[2:]
    if save:
        (qkv_o, prob_o, ctx_o, n1_o, r1_o, first_o, hid_o, slope_o, n2_o, r2_o) = refs[:10]
        refs = refs[10:]
    (x, wqkv, wout, wup, wdown, ctx, zbuf, first, hid, vec, bup) = refs[:11]
    refs = refs[11:]
    if save:
        (qkv, prob, n1, r1, slope, n2, r2) = refs[:7]
        refs = refs[7:]
    copies = Copies(refs[0])
    got_x = fetch_rows(copies, x_refs, x_kinds, x)
    pairs = [(w_refs[i], w_refs[4 + i] if len(sets) == 2 else w_refs[i]) for i in range(4)]
    got_qkv = copies.pick(pairs[0], wqkv)
    load_vectors(v_refs, sets, vec, bup)
    for cp in got_x:
        cp.wait()
    got_qkv.wait()
    got_out = copies.pick(pairs[1], wout)
    got_up = copies.pick(pairs[2], wup)
    got_down = copies.pick(pairs[3], wdown)
    keycol = lax.broadcasted_iota(jnp.int32, (1, SLOTS), 1)
    gain1, gain2 = vec[6:7], vec[7:8]

    def heads(i, carry):
        thirds = []
        for j in range(3):
            cols = pl.ds(pl.multiple_of(D * j + 256 * i, 256), 256)
            part = dot(x[...], wqkv[:, cols])
            if j != 1:
                at = pl.ds(pl.multiple_of(256 * i, 256), 256)
                part = part + vec[j // 2 : j // 2 + 1, at]
            part = part.astype(BF)
            if save:
                qkv[:, cols] = part
            thirds.append(part)
        for c in range(crops):
            crop = slice(SLOTS * c, SLOTS * (c + 1))
            for pr in range(2):
                qp, kp, vp = [t[crop, 128 * pr : 128 * (pr + 1)] for t in thirds]
                scores = jnp.where(keycol < lens[c], dot_nt(stack_heads(qp, 0.125), kp), MASKED)
                e = jnp.exp(scores - jnp.max(scores, axis=-1, keepdims=True))
                p = (e * pl.reciprocal(jnp.sum(e, axis=-1, keepdims=True))).astype(BF)
                if save:
                    prob[PAIRS * c + 2 * i + pr] = p
                at = pl.ds(pl.multiple_of(256 * i + 128 * pr, 128), 128)
                ctx[crop, at] = dot(side_by_side(p), stack_heads(vp, 1.0)).astype(BF)
        return carry

    lax.fori_loop(0, 3, heads, 0)
    if save:
        copies.send(qkv, qkv_o)
        copies.send(prob, prob_o)
        copies.send(ctx, ctx_o)
    got_out.wait()
    for j in range(3):
        cols = slice(256 * j, 256 * (j + 1))
        zbuf[:, cols] = x[:, cols].astype(F32) + dot(ctx[...], wout[:, cols]) + vec[2:3, cols]
    block = 64
    steps = rows // block

    def first_norm(i, carry):
        at = pl.ds(pl.multiple_of(i * block, block), block)
        n, r = norm_parts(zbuf[at, :])
        f = (n * gain1 + vec[3:4]).astype(BF)
        first[at, :] = f
        zbuf[at, :] = f.astype(F32) + vec[4:5]
        if save:
            n1[at, :] = n.astype(BF)
            r1[at, :] = jnp.broadcast_to(r, (block, 128))
        return carry

    lax.fori_loop(0, steps, first_norm, 0, unroll=True)
    if save:
        copies.send(n1, n1_o)
        copies.send(r1, r1_o)
        copies.send(first, first_o)
    got_up.wait()
    got_down.wait()

    def down_part(k):
        cols = slice(512 * k, 512 * (k + 1))
        zbuf[...] += dot(hid[:, cols], wdown[cols, :])

    for i in range(12):
        cols = slice(256 * i, 256 * (i + 1))
        g, slope_part = gelu_parts(dot(first[...], wup[:, cols]) + bup[:, cols], save)
        hid[:, cols] = g.astype(BF)
        if save:
            slope[:, cols] = slope_part.astype(BF)
        if i % 2 and i > 2:
            down_part(i // 2 - 1)
    if save:
        copies.send(hid, hid_o)
        copies.send(slope, slope_o)
    down_part(5)
    pool_ref[...] = jnp.zeros_like(pool_ref)
    per_crop = SLOTS // block
    for i in range(steps):
        at = slice(i * block, (i + 1) * block)
        n, r = norm_parts(zbuf[at, :])
        f = n * gain2 + vec[5:6]
        y_ref[at, :] = f.astype(BF)
        if save:
            n2[at, :] = n.astype(BF)
            r2[at, :] = jnp.broadcast_to(r, (block, 128))
        c = i // per_crop
        token = lax.broadcasted_iota(jnp.int32, (block, 1), 0) + (i % per_crop) * block
        part = jnp.sum(jnp.where(token < lens[c], f, 0.0), axis=0, keepdims=True)
        pool_ref[c : c + 1, :] += part / lens[c].astype(F32)
    if save:
        copies.send(n2, n2_o)
        copies.send(r2, r2_o)
    copies.drain()


def forward(rows, active, save, halves, whole, encoders):
    x_kinds = (("halves",) if halves else ()) + (("whole",) if whole is not None else ())
    xs = list(halves or ()) + ([whole] if whole is not None else [])
    lens = [e[1] for e in encoders]
    weights = [w for e in encoders for w in e[2]]
    vectors = [v for e in encoders for v in e[3]]
    outs = [((rows, D), BF), ((8, D), F32)]
    out_specs = [VMEM, VMEM]
    scratch = [
        ((rows, D), BF),
        ((D, 3 * D), BF),
        ((D, D), BF),
        ((D, FF), BF),
        ((FF, D), BF),
        ((rows, D), BF),
        ((rows, D), F32),
        ((rows, D), BF),
        ((rows, FF), BF),
        ((8, D), F32),
        ((1, FF), F32),
    ]
    if save:
        kept = saved_shapes(rows)
        outs += kept
        out_specs += [ANY] * len(kept)
        scratch += [kept[i] for i in (0, 1, 3, 4, 7, 8, 9)]
    return call(
        functools.partial(forward_kernel, rows, active, save, x_kinds, [e[0] for e in encoders]),
        "layer_forward",
        outs,
        out_specs,
        [*lens, *xs, *weights, *vectors],
        [SMEM] * len(lens) + [ANY] * (len(xs) + len(weights)) + [VMEM] * len(vectors),
        scratch,
        rows * 15000000,
        16000000 + (15000000 if save else 0),
    )


def split3(v):
    hi = v.astype(BF)
    rest = v - hi.astype(F32)
    mid = rest.astype(BF)
    lo = (rest - mid.astype(F32)).astype(BF)
    return hi, mid, lo


def stack3(v):
    parts = split3(v)
    return jnp.concatenate(list(parts) + [jnp.zeros_like(parts[0])] * 5, axis=0)


def unstack3(rows, n):
    return rows[:n] + rows[n : 2 * n] + rows[2 * n : 3 * n]


def queue_norm_kernel(active, queue_h, inv_ref, queue, sems):
    def run():
        Copies(sems).fetch(queue_h, queue).wait()

        def step(i, carry):
            at = pl.ds(pl.multiple_of(i * 512, 512), 512)
            v = queue[at, :].astype(F32)
            sq = v * v
            hi = sq.astype(BF)
            lo = (sq - hi.astype(F32)).astype(BF)
            ones = jnp.ones((8, D), BF)
            total = dot_nt(ones, hi) + dot_nt(ones, lo)
            inv_ref[:, at] = lax.rsqrt(total + 1e-6)
            return carry

        lax.fori_loop(0, queue.shape[0] // 512, step, 0)

    only_on(active, run)


def loss_kernel(active, crops, count, pooled, matched, queue, inv, grad_ref, loss_ref, sems):
    def run():
        v = pooled[:crops]
        r = lax.rsqrt(jnp.sum(v * v, axis=-1, keepdims=True) + 1e-6)
        u = v * r
        k = matched[:crops]
        near = jnp.sum(u * k, axis=-1, keepdims=True) * 20.0
        inv_row = inv[0:1]
        far = unstack3(dot_nt(stack3(u), queue[...]), crops) * (inv_row * 20.0)
        top = jnp.maximum(near, jnp.max(far, axis=-1, keepdims=True))
        e_near = jnp.exp(near - top)
        e_far = jnp.exp(far - top)
        total = e_near + jnp.sum(e_far, axis=-1, keepdims=True)
        share = 20.0 / (total * count)
        d_u = unstack3(dot(stack3(e_far * inv_row * share), queue[...]), crops)
        d_u = d_u + (e_near - total) * share * k
        grad = r * (d_u - u * jnp.sum(u * d_u, axis=-1, keepdims=True))
        grad_ref[...] = jnp.zeros_like(grad_ref)
        grad_ref[:crops] = grad
        lost = jnp.sum(top + jnp.log(total) - near, axis=0, keepdims=True) / count
        loss_ref[...] = jnp.broadcast_to(lost, loss_ref.shape)

    only_on(active, run)


def norm_back(dy, gain, n, r):
    dn = dy * gain
    return r * (dn - jnp.mean(dn, axis=-1, keepdims=True) - n * jnp.mean(dn * n, axis=-1, keepdims=True))


def column_sum(v):
    return jnp.sum(v, axis=0, keepdims=True)


def fast_mesh():
    return lax.axis_size("dp") == 8 and lax.axis_size("rep") == 2


def place_bits():
    dp, rep = lax.axis_index("dp"), lax.axis_index("rep")
    return dp // 2, dp % 2, rep


def norm_backward_kernel(rows, active, pooled, lens, dy, n2, r2, gains, ddown_ref, dsum_ref, vec_ref, sems):
    def run():
        gain = gains[0].astype(F32)[1:2]
        vec_ref[...] = jnp.zeros_like(vec_ref)
        block = 64
        per_crop = SLOTS // block
        for i in range(rows // block):
            at = slice(block * i, block * (i + 1))
            c = i // per_crop
            if pooled:
                token = lax.broadcasted_iota(jnp.int32, (block, 1), 0) + (i % per_crop) * block
                grow = jnp.where(token < lens[c], 1.0 / lens[c].astype(F32), 0.0) * dy[c : c + 1]
            else:
                grow = dy[at].astype(F32)
            n = n2[at].astype(F32)
            ds = norm_back(grow, gain, n, r2[at, 0:1])
            low = ds.astype(BF)
            dsum_ref[at] = ds
            ddown_ref[at] = low
            vec_ref[0:1] += column_sum(grow * n)
            vec_ref[1:2] += column_sum(grow)
            vec_ref[2:3] += column_sum(low.astype(F32))

    only_on(active, run)


def norm_backward(active, pooled, lens, dy, n2, r2, gains):
    rows = n2.shape[0]
    return call(
        functools.partial(norm_backward_kernel, rows, active, pooled),
        "second_norm_backward",
        [((rows, D), BF), ((rows, D), F32), ((8, D), F32)],
        [VMEM] * 3,
        [lens, dy, n2, r2, gains],
        [SMEM] + [VMEM] * 4,
        [],
        rows * 30 * D,
        5000000,
    )


CHUNK = 512


def ffn_backward_kernel(rows, active, ddown, dsum2, n1, r1, gains, slope_h, wdown_h, wup_h, *refs):
    def run():
        datt_ref, dsum_ref, vec_ref, bup_ref, dup_h, slope, wdown, wup, acc, dup, sems = refs
        copies = Copies(sems)
        got = []
        for i in range(FF // CHUNK):
            cols = slice(CHUNK * i, CHUNK * (i + 1))
            got.append(
                [
                    copies.fetch(wdown_h.at[cols, :], wdown.at[cols, :]),
                    copies.fetch(slope_h.at[:, cols], slope.at[:, cols]),
                    copies.fetch(wup_h.at[:, cols], wup.at[:, cols]),
                ]
            )
        vec_ref[...] = jnp.zeros_like(vec_ref)
        acc[...] = dsum2[...]
        for i in range(FF // CHUNK):
            cols = slice(CHUNK * i, CHUNK * (i + 1))
            for cp in got[i]:
                cp.wait()
            up = (dot_nt(ddown[...], wdown[cols, :]) * slope[:, cols].astype(F32)).astype(BF)
            dup[:, cols] = up
            copies.send(dup.at[:, cols], dup_h.at[:, cols])
            bup_ref[:, cols] = jnp.broadcast_to(column_sum(up.astype(F32)), (8, CHUNK))
            acc[...] += dot_nt(up, wup[:, cols])
        gain = gains[0].astype(F32)[0:1]
        block = 64
        for i in range(rows // block):
            at = slice(block * i, block * (i + 1))
            n = n1[at].astype(F32)
            dfirst = acc[at]
            ds = norm_back(dfirst, gain, n, r1[at, 0:1])
            low = ds.astype(BF)
            dsum_ref[at] = ds
            datt_ref[at] = low
            vec_ref[0:1] += column_sum(dfirst * n)
            vec_ref[1:2] += column_sum(dfirst)
            vec_ref[2:3] += column_sum(low.astype(F32))
        copies.drain()

    only_on(active, run)


def ffn_backward(active, ddown, dsum2, n1, r1, gains, slope, wdown, wup):
    rows = n1.shape[0]
    return call(
        functools.partial(ffn_backward_kernel, rows, active),
        "ffn_backward",
        [((rows, D), BF), ((rows, D), F32), ((8, D), F32), ((8, FF), F32), ((rows, FF), BF)],
        [VMEM] * 4 + [ANY],
        [ddown, dsum2, n1, r1, gains, slope, wdown, wup],
        [VMEM] * 5 + [ANY] * 3,
        [((rows, FF), BF), ((FF, D), BF), ((D, FF), BF), ((rows, D), F32), ((rows, FF), BF)],
        rows * 4 * FF * D,
        24000000,
    )


def ffn_weights_kernel(rows, active, fast, *refs):
    def run():
        if fast:
            first_h, first_p, ddown_h, ddown_p, hid_h, dup_h, wup_h, wdown_h, bup_h, send, keep = refs[:11]
            first, ddown, hid, dup, gup, gdown, wup, wdown, bup, sems = refs[11:]
        else:
            first_h, ddown_h, hid_h, dup_h, up_o, down_o = refs[:6]
            first, ddown, hid, dup, gup, gdown, sems = refs[6:]
        copies = Copies(sems)
        own = slice(0, rows)
        got = [copies.fetch(first_h, first.at[own, :]), copies.fetch(ddown_h, ddown.at[own, :])]
        z, x, y = place_bits()
        parts = 4 if fast else FF // 384
        if fast:
            peer = slice(rows, 2 * rows)
            got += [copies.fetch(first_p, first.at[peer, :]), copies.fetch(ddown_p, ddown.at[peer, :])]
            got.append(copies.fetch(bup_h, bup))
        blocks = []
        for i in range(parts):
            here = slice(384 * i, 384 * (i + 1))
            there = pl.ds(pl.multiple_of(768 * i + 384 * x, 128), 384) if fast else here
            block = [
                copies.fetch(hid_h.at[:, there], hid.at[own, here]),
                copies.fetch(dup_h.at[:, there], dup.at[own, here]),
            ]
            if fast:
                block.append(copies.fetch(wup_h.at[:, there], wup.at[:, here]))
                block.append(copies.fetch(wdown_h.at[there, :], wdown.at[here, :]))
            blocks.append(block)
        for cp in got:
            cp.wait()
        for i in range(parts):
            here = slice(384 * i, 384 * (i + 1))
            for cp in blocks[i]:
                cp.wait()
            if fast:
                there = pl.ds(pl.multiple_of(768 * i + 384 * x, 128), 384)
                bias = bup[:, there].astype(F32)
                g, slope = gelu_parts(dot(first[peer, :], wup[:, here]) + bias, True)
                hid[peer, here] = g.astype(BF)
                dup[peer, here] = (dot_nt(ddown[peer, :], wdown[here, :]) * slope).astype(BF)
            gdown[here, :] = dot_tn(hid[:, here], ddown[...]).astype(BF)
            gup[:, here] = dot_tn(first[...], dup[:, here]).astype(BF)
        if not fast:
            copies.send(gup, up_o)
            copies.send(gdown, down_o)
        else:
            for jy in (1, 0):
                out = send if jy else keep
                for jz in (3, 2, 1, 0):
                    zz, yy = jnp.bitwise_xor(z, jz), jnp.bitwise_xor(y, jy)
                    for jx in range(2):
                        owner = (zz * 2 + jnp.bitwise_xor(x, jx)) * 2 + yy
                        at = pl.ds(pl.multiple_of(48 * owner, 16), 48)
                        for c in range(2):
                            copies.send(
                                gup.at[at, slice(768 * c, 768 * (c + 1))],
                                out.at[jz, slice(96 * jx + 48 * c, 96 * jx + 48 * (c + 1)), :],
                            )
                    at = pl.ds(pl.multiple_of(384 * zz + 192 * yy, 64), 192)
                    copies.send(gdown.at[at, :], out.at[jz, 192:384, :])
        copies.drain()

    only_on(active, run)


def ffn_weights(active, first, first_peer, ddown, ddown_peer, hid, dup, wup, wdown, bup):
    rows = first.shape[0]
    fast = fast_mesh()
    if fast:
        ins = [first, first_peer, ddown, ddown_peer, hid, dup, wup, wdown, bup]
        outs = [((4, 384, D), BF)] * 2
        tokens, units = 2 * rows, FF // 2
        extra = [((D, units), BF), ((units, D), BF), ((1, FF), BF)]
    else:
        ins = [first, ddown, hid, dup]
        outs = [((D, FF), BF), ((FF, D), BF)]
        tokens, units, extra = rows, FF, []
    return call(
        functools.partial(ffn_weights_kernel, rows, active, fast),
        "ffn_weights",
        outs,
        [ANY] * 2,
        ins,
        [ANY] * len(ins),
        [
            ((tokens, D), BF),
            ((tokens, D), BF),
            ((tokens, units), BF),
            ((tokens, units), BF),
            ((D, units), BF),
            ((units, D), BF),
        ]
        + extra,
        rows * 6 * FF * D,
        20000000,
    )


def attention_backward_kernel(rows, active, datt, dsum1, qkv_h, prob_h, wout_h, wqkv_h, *refs):
    def run():
        dx_ref, vec_ref, dqkv_o, qkv, prob, wout, wqkv, dqkv, sems = refs
        copies = Copies(sems)
        got_out = copies.fetch(wout_h, wout)
        got_qkv = copies.fetch(qkv_h, qkv)
        got_prob = copies.fetch(prob_h, prob)
        got_w = copies.fetch(wqkv_h, wqkv)
        got_out.wait()
        dctx = dot_nt(datt[...], wout[...]).astype(BF)
        got_qkv.wait()
        got_prob.wait()
        for c in range(rows // SLOTS):
            crop = slice(SLOTS * c, SLOTS * (c + 1))
            for pr in range(PAIRS):
                cols = [slice(D * j + 128 * pr, D * j + 128 * (pr + 1)) for j in range(3)]
                qp, kp, vp = [qkv[crop, t] for t in cols]
                dcs = stack_heads(dctx[crop, 128 * pr : 128 * (pr + 1)], 1.0)
                p = prob[PAIRS * c + pr]
                pf = p.astype(F32)
                weighted = pf * dot_nt(dcs, vp)
                ds = (weighted - pf * jnp.sum(weighted, axis=-1, keepdims=True)).astype(BF)
                dqkv[crop, cols[0]] = dot(side_by_side(ds), stack_heads(kp, 0.125)).astype(BF)
                dqkv[crop, cols[1]] = dot_tn(ds, stack_heads(qp, 0.125)).astype(BF)
                dqkv[crop, cols[2]] = dot_tn(p, dcs).astype(BF)
        copies.send(dqkv, dqkv_o)
        vec_ref[...] = jnp.zeros_like(vec_ref)
        vec_ref[0:1] = column_sum(dqkv[:, :D].astype(F32))
        vec_ref[1:2] = column_sum(dqkv[:, 2 * D :].astype(F32))
        got_w.wait()
        for j in range(3):
            cols = slice(256 * j, 256 * (j + 1))
            dx_ref[:, cols] = (dot_nt(dqkv[...], wqkv[cols, :]) + dsum1[:, cols]).astype(BF)
        copies.drain()

    only_on(active, run)


def attention_backward(active, datt, dsum1, qkv, prob, wout, wqkv):
    rows = datt.shape[0]
    return call(
        functools.partial(attention_backward_kernel, rows, active),
        "attention_backward",
        [((rows, D), BF), ((8, D), F32), ((rows, 3 * D), BF)],
        [VMEM] * 2 + [ANY],
        [datt, dsum1, qkv, prob, wout, wqkv],
        [VMEM] * 2 + [ANY] * 4,
        [(qkv.shape, BF), (prob.shape, BF), (wout.shape, BF), (wqkv.shape, BF), (qkv.shape, BF)],
        rows * (4 * D * D * 2 + 10 * SLOTS * D),
        22000000,
    )


def attention_weights_kernel(rows, active, fast, x_kinds, *refs):
    def run():
        n_x = len(x_kinds) + 1
        x_refs = refs[:n_x]
        ctx_h, datt_h, dqkv_h, out_a, out_b, x, ctx, datt, dqkv, gqkv, gout, sems = refs[n_x:]
        copies = Copies(sems)
        got = [copies.fetch(ctx_h, ctx), copies.fetch(datt_h, datt)]
        got_x = fetch_rows(copies, x_refs, x_kinds, x)
        got_x.append(copies.fetch(dqkv_h, dqkv))
        for cp in got:
            cp.wait()
        gout[...] = dot_tn(ctx[...], datt[...]).astype(BF)
        for cp in got_x:
            cp.wait()
        for j in range(6):
            cols = slice(384 * j, 384 * (j + 1))
            gqkv[:, cols] = dot_tn(x[...], dqkv[:, cols]).astype(BF)
        if not fast:
            copies.send(gqkv, out_a)
            copies.send(gout, out_b)
        else:
            z, xx, y = place_bits()
            for j in range(15, -1, -1):
                jx, jy, jz = j // 8, j // 4 % 2, j % 4
                owner = (jnp.bitwise_xor(z, jz) * 2 + jnp.bitwise_xor(xx, jx)) * 2 + jnp.bitwise_xor(y, jy)
                at = pl.ds(pl.multiple_of(48 * owner, 16), 48)
                out = (out_b if jx else out_a).at[j % 8]
                for t in range(3):
                    copies.send(gqkv.at[at, slice(D * t, D * (t + 1))], out.at[48 * t : 48 * (t + 1), :])
                copies.send(gout.at[at, :], out.at[144:192, :])
        copies.drain()

    only_on(active, run)


def attention_weights(active, halves, whole, ctx, datt, dqkv):
    rows = ctx.shape[0]
    fast = fast_mesh()
    x_kinds = ("halves", "whole")
    outs = [((8, 192, D), BF)] * 2 if fast else [((D, 3 * D), BF), ((D, D), BF)]
    ins = [*halves, whole, ctx, datt, dqkv]
    return call(
        functools.partial(attention_weights_kernel, rows, active, fast, x_kinds),
        "attention_weights",
        outs,
        [ANY] * 2,
        ins,
        [ANY] * len(ins),
        [((rows, D), BF)] * 3 + [((rows, 3 * D), BF), ((D, 3 * D), BF), ((D, D), BF)],
        rows * 8 * D * D,
        12000000,
    )


AXES = ("section", "dp", "rep")


def swap(block, section, dp_flip, rep_flip):
    dps, reps = lax.axis_size("dp"), lax.axis_size("rep")
    sections = range(lax.axis_size("section")) if section is None else [section]
    route = [
        ((s * dps + d) * reps + r, (s * dps + (d ^ dp_flip)) * reps + (r ^ rep_flip))
        for s in sections
        for d in range(dps)
        for r in range(reps)
    ]
    return lax.ppermute(block, AXES, route)


def flips():
    out, bit = [], 1
    while bit < lax.axis_size("rep"):
        out.append((0, bit))
        bit *= 2
    bit = 1
    while bit < lax.axis_size("dp"):
        out.append((bit, 0))
        bit *= 2
    return out


def low(v):
    return v.astype(BF)


def wide(*terms):
    total = terms[0].astype(F32)
    for t in terms[1:]:
        total = total + t.astype(F32)
    return total


def attention_sum(keep, send, section):
    first = swap(send, section, 1, 0)
    second = swap(low(wide(keep[4:], first[4:])), section, 0, 1)
    parts = [wide(keep[k], first[k], second[k]) for k in range(4)]
    others = [swap(low(parts[k]), section, 2 * k, 0) for k in range(1, 4)]
    return wide(parts[0], *others)


def ffn_sum(keep, send, section):
    first = swap(send, section, 0, 1)
    parts = [wide(keep[k], first[k]) for k in range(4)]
    others = [swap(low(parts[k]), section, 2 * k, 0) for k in range(1, 4)]
    return wide(parts[0], *others)


def body(
    query_crops,
    key_crops,
    query_lengths,
    key_lengths,
    positive,
    queue,
    qkv_weight,
    out_weight,
    up_weight,
    down_weight,
    biases,
    gains,
    up_biases,
    query_bias,
    key_qkv_weight,
    key_out_weight,
    key_up_weight,
    key_down_weight,
    key_biases,
    key_gains,
    key_up_biases,
):
    crops = query_crops.shape[0]
    rows = crops * SLOTS
    sections, dps, reps = [lax.axis_size(a) for a in AXES]
    fast = fast_mesh()
    crop_all = crops * dps * reps
    on_first = lax.axis_index("section") == 0
    dp, rep = lax.axis_index("dp"), lax.axis_index("rep")
    last = sections - 1

    def relay(block, distance):
        return lax.ppermute(block, "section", [(0, 1)] if distance > 0 else [(1, 0)])

    key_halves = (key_crops, relay(key_crops, -1))
    query_halves = (query_crops, relay(query_crops, -1))
    query_weights = [w[0] for w in (qkv_weight, out_weight, up_weight, down_weight)]
    key_weights = [w[0] for w in (key_qkv_weight, key_out_weight, key_up_weight, key_down_weight)]
    query_encoder = ("query", query_lengths, query_weights, (biases, gains, up_biases, query_bias))
    key_encoder = ("key", key_lengths, key_weights, (key_biases, key_gains, key_up_biases))

    key_middle, _ = forward(rows, 0, False, key_halves, None, [key_encoder])
    inv = call(
        functools.partial(queue_norm_kernel, last),
        "queue_norm",
        [((8, queue.shape[0]), F32)],
        [VMEM],
        [queue],
        [ANY],
        [(queue.shape, BF)],
        8 * queue.size,
        queue.size * 2,
    )[0]
    key_middle, inv = lax.optimization_barrier((key_middle, inv))
    key_middle = relay(key_middle, 1)
    query_middle, key_pooled = forward(rows, None, False, query_halves, key_middle, [query_encoder, key_encoder])
    query_middle = relay(query_middle, 1)

    every_key = key_pooled[:crops]
    every_key = every_key * lax.rsqrt(jnp.sum(every_key * every_key, axis=-1, keepdims=True) + 1e-6)
    near_flips = [(0, 1), (1, 0), (1, 1)]
    if fast:
        every_key = jnp.concatenate([every_key] + [swap(every_key, None, *f) for f in near_flips], axis=0)
    step = forward(rows, None, True, query_halves, query_middle, [query_encoder])
    query_pooled = step[1]
    qkv, prob, ctx, n1, r1, first, hid, slope, n2, r2 = step[2:]

    if fast:
        every_key, query_pooled = lax.optimization_barrier((every_key, query_pooled))
        every_key = jnp.concatenate([every_key] + [swap(every_key, None, 2 * k, 0) for k in range(1, 4)], axis=0)
    else:
        for flip in flips():
            every_key = jnp.concatenate([every_key, swap(every_key, None, *flip)], axis=0)
    place = dp * reps + rep
    matched = jnp.take(every_key, jnp.bitwise_xor(positive // crops, place) * crops + positive % crops, axis=0)
    matched = jnp.concatenate([matched, jnp.zeros((8 - crops, D), F32)], axis=0)
    first_peer = swap(first, None, 1, 0) if fast else None

    pooled_grad, lost = call(
        functools.partial(loss_kernel, last, crops, crop_all),
        "contrast",
        [((8, D), F32), ((8, 128), F32)],
        [VMEM] * 2,
        [query_pooled, matched, queue, inv],
        [VMEM] * 4,
        [],
        16 * 2 * queue.size,
        queue.size * 2,
    )

    def ffn_part(active, pooled, dy):
        ddown, dsum2, vec_a = norm_backward(active, pooled, query_lengths, dy, n2, r2, gains)
        ddown_peer = swap(ddown, active, 1, 0) if fast else None
        datt, dsum1, vec_b, grad_bup, dup = ffn_backward(
            active, ddown, dsum2, n1, r1, gains, slope, query_weights[3], query_weights[2]
        )
        return ddown, ddown_peer, dup, datt, dsum1, vec_a, vec_b, grad_bup

    def ffn_grads(active, ddown, ddown_peer, dup):
        return ffn_weights(
            active, first, first_peer, ddown, ddown_peer, hid, dup, query_weights[2], query_weights[3], up_biases
        )

    def attention_part(active, datt, dsum1):
        return attention_backward(active, datt, dsum1, qkv, prob, query_weights[1], query_weights[0])

    def attention_grads(active, datt, dqkv):
        return attention_weights(active, query_halves, query_middle, ctx, datt, dqkv)

    def small_rows(vec_a, vec_b, vec_c, grad_bup):
        picked = [vec_c[1:2], vec_b[2:3], vec_b[1:2], vec_a[2:3], vec_a[1:2], vec_b[0:1], vec_a[0:1], vec_c[0:1]]
        return jnp.concatenate(picked + [grad_bup[0:1].reshape(FF // D, D)], axis=0)

    ddown, ddown_peer, dup, datt, dsum1, vec_a, vec_b, grad_bup = ffn_part(last, True, pooled_grad)
    dmiddle, vec_c, dqkv = attention_part(last, datt, dsum1)
    small_last = small_rows(vec_a, vec_b, vec_c, grad_bup)
    dmiddle = relay(dmiddle, -1)
    attention_last = attention_grads(last, datt, dqkv)
    ffn_last = ffn_grads(last, ddown, ddown_peer, dup)

    ddown, ddown_peer, dup, datt, dsum1, vec_a, vec_b, grad_bup = ffn_part(0, False, dmiddle)
    ffn_first = ffn_grads(0, ddown, ddown_peer, dup)
    dx, vec_c, dqkv = attention_part(0, datt, dsum1)
    small_first = small_rows(vec_a, vec_b, vec_c, grad_bup)
    attention_first = attention_grads(0, datt, dqkv)

    if fast:
        attention_total = [attention_sum(*attention_first, 0), attention_sum(*attention_last, last)]
        ffn_total = [ffn_sum(ffn_first[1], ffn_first[0], 0), ffn_sum(ffn_last[1], ffn_last[0], last)]
        attention_total = jnp.where(on_first, *attention_total)
        ffn_total = jnp.where(on_first, *ffn_total)
        grad_qkv = jnp.concatenate([attention_total[48 * t : 48 * (t + 1)] for t in range(3)], axis=1)
        grad_out = attention_total[144:]
        grad_down = ffn_total[192:]

        def joined(rows96):
            return jnp.concatenate([rows96[:48], rows96[48:96]], axis=1).reshape(48, 4, 384)

        own = joined(ffn_total[:96])
        peer = swap(joined(ffn_total[96:192]), None, 1, 0)
        even = dp % 2 == 0
        grad_up = jnp.stack([jnp.where(even, own, peer), jnp.where(even, peer, own)], axis=2).reshape(48, FF)
    else:
        totals = [
            lax.psum_scatter(jnp.where(on_first, a, b).astype(F32), ("dp", "rep"), scatter_dimension=0, tiled=True)
            for a, b in zip([*ffn_first, *attention_first], [*ffn_last, *attention_last])
        ]
        grad_up, grad_down, grad_qkv, grad_out = totals

    small = jnp.where(on_first, small_first, small_last)
    loss_row = jnp.where(on_first, 0.0, jnp.concatenate([lost[0:1]] * (D // 128), axis=1))
    small = jnp.concatenate([small, loss_row], axis=0)
    for flip in flips():
        small = small + swap(small, None, *flip)
    loss_value = jnp.where(on_first, relay(small[12, :128], -1), small[12, :128])[:1]
    width = D // (dps * reps)
    mine = lax.dynamic_slice(small[:8], (0, place * width), (8, width))
    up_part = lax.dynamic_slice(small[8:12].reshape(FF), (place * (FF // (dps * reps)),), (FF // (dps * reps),))

    dx = dx.reshape(crops, SLOTS, D)
    half = SLOTS // sections
    crops_grad = jnp.where(on_first, dx[:, :half], lax.ppermute(dx[:, half:], "section", [(0, 1)])).astype(F32)
    return (
        loss_value,
        crops_grad,
        grad_qkv[None],
        grad_out[None],
        grad_up[None],
        grad_down[None],
        mine[None, :5],
        mine[None, 5:7],
        up_part[None],
        mine[None, 7],
    )


def solution(mesh):
    crop = P(("dp", "rep"), "section", None)
    per_crop = P(("dp", "rep"))
    layer3 = P("section", None, None)
    layer2 = P("section", None)
    placed = (
        (crop, crop, per_crop, per_crop, per_crop, P())
        + (layer3,) * 6
        + (layer2,) * 2
        + (layer3,) * 6
        + (layer2,)
    )
    shared3 = P("section", ("dp", "rep"), None)
    return jax.shard_map(
        body,
        mesh=mesh,
        in_specs=placed,
        out_specs=(
            P(),
            crop,
            shared3,
            shared3,
            shared3,
            shared3,
            P("section", None, ("dp", "rep")),
            P("section", None, ("dp", "rep")),
            P("section", ("dp", "rep")),
            P("section", ("dp", "rep")),
        ),
        check_vma=False,
    )
```

profile of v0, /device:TPU:0, one launch (start us, length us, event | category | flops | bytes accessed | tf_op | source)
XLA Modules:
  0.0 388.7 jit_solution(11527604197031714777)
XLA Ops:
  0.6 1.3 collective-permute-start.1
  1.9 1.5 queue_norm.1.inv
  5.2 21.3 %layer_forward.3 = (bf16[512,768]{1,0:T(8,128)(2,1)}, f32[8,768]{1,0:T(8,128)}) custom-call(s32[2]{0:T(128)} %refs_1_.4, bf16[2,128,768]{2,1,0:T(8,128)(2,1)} %refs_1_.3, bf16[2,128,768]{2,1,0:T(8,128)(2,1)} %copy-done.18, bf16[768,2304]{1,0:T(8,128)(2,1)} %bitcast.100, bf16[768,768]{1,0:T(8,128)(2,1)} %bitcast.106, bf16[768,3072]{1,0:T(8,128)(2,1)} %bitcast.84, ...), custom_call_target="tpu_custom_call" | custom-call | flops 7680000000 | bytes 16000000 | tf_op jit(solution)/shard_map/layer_forward/pallas_call | solution.py:125
  26.6 1.3 collective-permute-start.2
  27.9 1.5 collective-permute-start
  29.5 2.1 collective-permute-done.refs_3_.refs_2_.refs_1_
  32.5 21.3 %layer_forward.4 = (bf16[512,768]{1,0:T(8,128)(2,1)}, f32[8,768]{1,0:T(8,128)}) custom-call(s32[2]{0:T(128)} %lens.3, s32[2]{0:T(128)} %refs_1_.4, bf16[2,128,768]{2,1,0:T(8,128)(2,1)} %refs_0_.9, bf16[2,128,768]{2,1,0:T(8,128)(2,1)} %copy-done.11, bf16[512,768]{1,0:T(8,128)(2,1)} %copy-done.8, bf16[768,2304]{1,0:T(8,128)(2,1)} %bitcast.102, ...), custom_call_target="tpu_custom_call" | custom-call | flops 7680000000 | bytes 16000000 | tf_op jit(solution)/shard_map/layer_forward/pallas_call | solution.py:125
  53.9 2.1 collective-permute-start.6
  57.6 3.9 %collective-permute-start.5 = (f32[2,768]{1,0:T(2,128)S(1)}, f32[2,768]{1,0:T(2,128)S(1)}, u32[]{:S(2)}, u32[]{:S(2)}) collective-permute-start(f32[2,768]{1,0:T(2,128)S(1)} %slice_multiply_fusion), channel_id=1, source_target_pairs={{0,3},{1,2},{2,1},{3,0},{4,7},{5,6},{6,5},{7,4},{8,11},{9,10},{10,... | collective-permute-start | bytes 18440 | tf_op jit(solution)/shard_map/ppermute | solution.py:774
  63.1 2.0 collective-permute-done.4
  66.6 35.1 %layer_forward.5 = (bf16[512,768]{1,0:T(8,128)(2,1)}, f32[8,768]{1,0:T(8,128)}, bf16[512,2304]{1,0:T(8,128)(2,1)}, bf16[12,512,256]{2,1,0:T(8,128)(2,1)}, bf16[5...) custom-call(s32[2]{0:T(128)} %lens.3, ...), custom_call_target="tpu_custom_call" | custom-call | flops 7680000000 | bytes 31000000 | tf_op jit(solution)/shard_map/layer_forward/pallas_call | solution.py:125
  101.7 3.7 collective-permute-start.9
  106.1 1.5 collective-permute-start.27
  107.6 2.4 collective-permute-done.8
  111.3 4.5 %contrast.1 = (f32[8,768]{1,0:T(8,128)}, f32[8,128]{1,0:T(8,128)}) custom-call(f32[8,768]{1,0:T(8,128)} %get-tuple-element.65.pooled, f32[8,768]{1,0:T(8,128)} %concatenate.40.matched, bf16[4096,768]{1,0:T(8,128)(2,1)} %queue.1, f32[8,4096]{1,0:T(8,128)} %queue_norm.1.inv), custom_call_target="tpu_custom_call" | custom-call | flops 100663296 | bytes 6291456 | tf_op jit(solution)/shard_map/contrast/pallas_call | solution.py:125
  117.9 3.5 second_norm_backward.2
  122.1 4.3 %ffn_backward.2 = (bf16[512,768]{1,0:T(8,128)(2,1)}, f32[512,768]{1,0:T(8,128)}, f32[8,768]{1,0:T(8,128)}, f32[8,3072]{1,0:T(8,128)}, bf16[512,3072]{1,0:T(8,128)(2,1)}) custom-call(bf16[512,768]{1,0:T(8,128)(2,1)} %get-tuple-element.71.ddown.refs_2_, f32[512,768]{1,0:T(8,128)} %get-tuple-element.72.dsum2, bf16[512,768]{1,0:T(8,128)(2,1)} %get-tuple-element.73.n1, ...), custom_call_target="tpu_custom_call" | custom-call | flops 4831838208 | bytes 24000000 | tf_op jit(solution)/shard_map/ffn_backward/pallas_call | solution.py:125
  126.4 3.8 attention_backward.2
  130.2 1.3 collective-permute-start.10
  135.9 2.1 collective-permute-start.22
  140.1 17.5 %collective-permute-done.10.dy = bf16[512,768]{1,0:T(8,128)(2,1)S(1)} collective-permute-done((bf16[512,768]{1,0:T(8,128)(2,1)}, bf16[512,768]{1,0:T(8,128)(2,1)S(1)}, u32[]{:S(2)}, u32[]{:S(2)}) %collective-permute-start.10) | collective-permute-done | bytes 786464 | tf_op jit(solution)/shard_map/ppermute | solution.py:848
  158.5 5.1 %second_norm_backward.3 = (bf16[512,768]{1,0:T(8,128)(2,1)}, f32[512,768]{1,0:T(8,128)}, f32[8,768]{1,0:T(8,128)}) custom-call(s32[2]{0:T(128)} %lens.3, bf16[512,768]{1,0:T(8,128)(2,1)} %copy-done.5, bf16[512,768]{1,0:T(8,128)(2,1)} %get-tuple-element.69.n2, f32[512,128]{1,0:T(8,128)} %get-tuple-element.70.r2, bf16[1,2,768]{2,1,0:T(2,128)(2,1)} %gains.7), custom_call_target="tpu_custom_call" | custom-call | flops 11796480 | bytes 5000000 | tf_op jit(solution)/shard_map/second_norm_backward/pallas_call | solution.py:125
  163.6 2.4 collective-permute-start.28
  166.1 13.6 %ffn_backward.3 = (bf16[512,768]{1,0:T(8,128)(2,1)}, f32[512,768]{1,0:T(8,128)}, f32[8,768]{1,0:T(8,128)}, f32[8,3072]{1,0:T(8,128)}, bf16[512,3072]{1,0:T(8,128)(2,1)}) custom-call(bf16[512,768]{1,0:T(8,128)(2,1)} %get-tuple-element.81.ddown.refs_2_, f32[512,768]{1,0:T(8,128)} %get-tuple-element.82.dsum2, bf16[512,768]{1,0:T(8,128)(2,1)} %get-tuple-element.73.n1, ...), custom_call_target="tpu_custom_call" | custom-call | flops 4831838208 | bytes 24000000 | tf_op jit(solution)/shard_map/ffn_backward/pallas_call | solution.py:125
  180.6 14.6 %attention_backward.3 = (bf16[512,768]{1,0:T(8,128)(2,1)}, f32[8,768]{1,0:T(8,128)}, bf16[512,2304]{1,0:T(8,128)(2,1)}) custom-call(bf16[512,768]{1,0:T(8,128)(2,1)} %get-tuple-element.83.datt.refs_4_, f32[512,768]{1,0:T(8,128)} %get-tuple-element.84.dsum1, bf16[512,2304]{1,0:T(8,128)(2,1)} %get-tuple-element.78.qkv_h, ...), custom_call_target="tpu_custom_call" | custom-call | flops 3422552064 | bytes 22000000 | tf_op jit(solution)/shard_map/attention_backward/pallas_call | solution.py:125
  195.2 8.1 %attention_weights.2 = (bf16[8,192,768]{2,1,0:T(8,128)(2,1)}, bf16[8,192,768]{2,1,0:T(8,128)(2,1)}) custom-call(bf16[2,128,768]{2,1,0:T(8,128)(2,1)} %refs_0_.9, bf16[2,128,768]{2,1,0:T(8,128)(2,1)} %copy-done.11, bf16[512,768]{1,0:T(8,128)(2,1)} %copy-done.14, bf16[512,768]{1,0:T(8,128)(2,1)} %get-tuple-element.95.refs_3_, ...), custom_call_target="tpu_custom_call" | custom-call | flops 2415919104 | bytes 12000000 | tf_op jit(solution)/shard_map/attention_weights/pallas_call | solution.py:125
  203.3 3.4 collective-permute-start.17
  207.9 1.2 ffn_weights.3
  209.1 2.1 collective-permute-start.34
  214.7 19.6 %ffn_weights.2 = (bf16[4,384,768]{2,1,0:T(8,128)(2,1)}, bf16[4,384,768]{2,1,0:T(8,128)(2,1)}) custom-call(bf16[512,768]{1,0:T(8,128)(2,1)} %get-tuple-element.102.refs_0_, bf16[512,768]{1,0:T(8,128)(2,1)} %copy-done.15, bf16[512,768]{1,0:T(8,128)(2,1)} %get-tuple-element.81.ddown.refs_2_, bf16[512,768]{1,0:T(8,128)(2,1)} %copy-done.17, ...), custom_call_target="tpu_custom_call" | custom-call | flops 7247757312 | bytes 20000000 | tf_op jit(solution)/shard_map/ffn_weights/pallas_call | solution.py:125
  234.3 2.1 collective-permute-start.29
  236.5 1.9 collective-permute-start.11
  238.3 34.6 %collective-permute-done.11 = f32[13,768]{1,0:T(8,128)S(1)} collective-permute-done((f32[13,768]{1,0:T(8,128)S(1)}, f32[13,768]{1,0:T(8,128)S(1)}, u32[]{:S(2)}, u32[]{:S(2)}) %collective-permute-start.11) | collective-permute-done | bytes 39968 | tf_op jit(solution)/shard_map/ppermute | solution.py:774
  273.5 3.5 collective-permute-done.12
  277.2 4.1 %collective-permute-done.13 = f32[13,768]{1,0:T(8,128)S(1)} collective-permute-done((f32[13,768]{1,0:T(8,128)S(1)}, f32[13,768]{1,0:T(8,128)S(1)}, u32[]{:S(2)}, u32[]{:S(2)}) %collective-permute-start.13) | collective-permute-done | bytes 39968 | tf_op jit(solution)/shard_map/ppermute | solution.py:774
  281.2 1.9 collective-permute-start.14
  284.0 2.3 collective-permute-done.14
  286.3 2.7 add_convert_fusion
  289.8 2.8 add_convert_fusion.1
  292.6 2.0 collective-permute-start.18
  295.2 1.3 collective-permute-start.15
  296.6 2.9 fusion.8
  299.5 1.7 collective-permute-start.37
  303.4 1.3 dynamic_slice.7
  304.8 4.9 %collective-permute-start.16 = (bf16[2,128,768]{2,1,0:T(8,128)(2,1)}, bf16[2,128,768]{2,1,0:T(8,128)(2,1)S(1)}, u32[]{:S(2)}, u32[]{:S(2)}) collective-permute-start(bf16[2,128,768]{2,1,0:T(8,128)(2,1)} %slice.339), channel_id=1, source_target_pairs={{0,16},{1,17},{2,18},{3,19},{4,20},{5,21},{6,22},{7,23},{8,24},{9,... | collective-permute-start | bytes 1179656 | tf_op jit(solution)/shard_map/ppermute | solution.py:977
  311.6 2.5 fusion.5
  314.8 4.1 %collective-permute-start.32 = (bf16[384,768]{1,0:T(8,128)(2,1)S(1)}, bf16[384,768]{1,0:T(8,128)(2,1)S(1)}, u32[]{:S(2)}, u32[]{:S(2)}) collective-permute-start(bf16[384,768]{1,0:T(8,128)(2,1)S(1)} %get-tuple-element.119), channel_id=1, source_target_pairs={{0,12},{1,13},{2,14},{3,15},{4,8},{5,9},{6,10},{7,11},{8,4},{9,5},... | collective-permute-start | bytes 1769480 | tf_op jit(solution)/shard_map/ppermute | solution.py:774
  318.9 2.3 collective-permute-start.31
  321.2 3.7 collective-permute-start.30
  325.9 2.3 fusion.20
  328.2 2.8 fusion.17
  331.0 1.4 collective-permute-start.26
  332.3 1.4 collective-permute-start.25
  334.7 1.4 collective-permute-start.24
  336.1 20.2 %collective-permute-done.31 = bf16[384,768]{1,0:T(8,128)(2,1)S(1)} collective-permute-done((bf16[384,768]{1,0:T(8,128)(2,1)S(1)}, bf16[384,768]{1,0:T(8,128)(2,1)S(1)}, u32[]{:S(2)}, u32[]{:S(2)}) %collective-permute-start.31) | collective-permute-done | bytes 589856 | tf_op jit(solution)/shard_map/ppermute | solution.py:774
  356.3 4.9 %collective-permute-start.21 = (bf16[192,768]{1,0:T(8,128)(2,1)}, bf16[192,768]{1,0:T(8,128)(2,1)}, u32[]{:S(2)}, u32[]{:S(2)}) collective-permute-start(bf16[192,768]{1,0:T(8,128)(2,1)} %get-tuple-element.113), channel_id=1, source_target_pairs={{0,12},{1,13},{2,14},{3,15},{4,8},{5,9},{6,10},{7,11},{8,4},{9,5},... | collective-permute-start | bytes 884744 | tf_op jit(solution)/shard_map/ppermute | solution.py:774
  361.3 1.9 collective-permute-start.20
  363.2 2.6 fusion.2
  366.6 3.2 collective-permute-start.19
  370.6 1.8 reshape.204
  372.4 1.8 reshape.205
  375.6 7.1 %collective-permute-done.20 = bf16[192,768]{1,0:T(8,128)(2,1)} collective-permute-done((bf16[192,768]{1,0:T(8,128)(2,1)}, bf16[192,768]{1,0:T(8,128)(2,1)}, u32[]{:S(2)}, u32[]{:S(2)}) %collective-permute-start.20) | collective-permute-done | bytes 294944 | tf_op jit(solution)/shard_map/ppermute | solution.py:774
  382.7 2.3 fusion.13
  387.2 1.3 broadcast_in_dim_reshape.3
  (134 shorter events, 40.0 us)
Async XLA Ops:
  0.6 3.8 collective-permute-start.1
  4.5 0.7 copy-start.18
  5.2 22.7 %copy-start.10 = (bf16[2,128,768]{2,1,0:T(8,128)(2,1)S(1)}, bf16[2,128,768]{2,1,0:T(8,128)(2,1)}, u32[]{:S(2)}) copy-start(bf16[2,128,768]{2,1,0:T(8,128)(2,1)} %refs_0_.9) | copy-start | bytes 1179652
  26.6 5.0 %collective-permute-start.2 = (bf16[512,768]{1,0:T(8,128)(2,1)}, bf16[512,768]{1,0:T(8,128)(2,1)S(1)}, u32[]{:S(2)}, u32[]{:S(2)}) collective-permute-start(bf16[512,768]{1,0:T(8,128)(2,1)} %get-tuple-element.61), channel_id=1, source_target_pairs={{0,16},{1,17},{2,18},{3,19},{4,20},{5,21},{6,22},{7,23},{8,24},{9,... | collective-permute-start | bytes 2359304 | tf_op jit(solution)/shard_map/ppermute | solution.py:848
  27.9 3.6 collective-permute-start
  31.5 0.7 copy-start.11
  31.5 1.0 copy-start.8
  32.5 29.5 %copy-start.13 = (s32[2]{0:T(128)S(1)}, s32[2]{0:T(128)}, u32[]{:S(2)}) copy-start(s32[2]{0:T(128)} %param.25) | copy-start | bytes 28
  53.9 11.9 %collective-permute-start.6 = (bf16[512,768]{1,0:T(8,128)(2,1)}, bf16[512,768]{1,0:T(8,128)(2,1)S(1)}, u32[]{:S(2)}, u32[]{:S(2)}) collective-permute-start(bf16[512,768]{1,0:T(8,128)(2,1)} %get-tuple-element.63), channel_id=1, source_target_pairs={{0,16},{1,17},{2,18},{3,19},{4,20},{5,21},{6,22},{7,23},{8,24},{9,... | collective-permute-start | bytes 2359304 | tf_op jit(solution)/shard_map/ppermute | solution.py:848
  57.6 5.5 %collective-permute-start.5 = (f32[2,768]{1,0:T(2,128)S(1)}, f32[2,768]{1,0:T(2,128)S(1)}, u32[]{:S(2)}, u32[]{:S(2)}) collective-permute-start(f32[2,768]{1,0:T(2,128)S(1)} %slice_multiply_fusion), channel_id=1, source_target_pairs={{0,3},{1,2},{2,1},{3,0},{4,7},{5,6},{6,5},{7,4},{8,11},{9,10},{10,... | collective-permute-start | bytes 18440 | tf_op jit(solution)/shard_map/ppermute | solution.py:774
  61.5 3.6 collective-permute-start.4
  62.1 3.6 collective-permute-start.3
  65.7 0.9 copy-start.14
  101.7 6.0 %collective-permute-start.9 = (f32[8,768]{1,0:T(8,128)S(1)}, f32[8,768]{1,0:T(8,128)S(1)}, u32[]{:S(2)}, u32[]{:S(2)}) collective-permute-start(f32[8,768]{1,0:T(8,128)S(1)} %pad_maximum_fusion.5), channel_id=1, source_target_pairs={{0,12},{1,13},{2,14},{3,15},{4,8},{5,9},{6,10},{7,11},{8,4},{9,5},... | collective-permute-start | bytes 73736 | tf_op jit(solution)/shard_map/ppermute | solution.py:774
  105.3 4.7 %collective-permute-start.8 = (f32[8,768]{1,0:T(8,128)S(1)}, f32[8,768]{1,0:T(8,128)S(1)}, u32[]{:S(2)}, u32[]{:S(2)}) collective-permute-start(f32[8,768]{1,0:T(8,128)S(1)} %pad_maximum_fusion.5), channel_id=1, source_target_pairs={{0,8},{1,9},{2,10},{3,11},{4,12},{5,13},{6,14},{7,15},{8,0},{9,1},... | collective-permute-start | bytes 73736 | tf_op jit(solution)/shard_map/ppermute | solution.py:774
  105.3 4.7 %collective-permute-start.7 = (f32[8,768]{1,0:T(8,128)S(1)}, f32[8,768]{1,0:T(8,128)S(1)}, u32[]{:S(2)}, u32[]{:S(2)}) collective-permute-start(f32[8,768]{1,0:T(8,128)S(1)} %pad_maximum_fusion.5), channel_id=1, source_target_pairs={{0,4},{1,5},{2,6},{3,7},{4,0},{5,1},{6,2},{7,3},{8,12},{9,13},{10,... | collective-permute-start | bytes 73736 | tf_op jit(solution)/shard_map/ppermute | solution.py:774
  106.1 100.6 %collective-permute-start.27 = (bf16[512,768]{1,0:T(8,128)(2,1)}, bf16[512,768]{1,0:T(8,128)(2,1)S(1)}, u32[]{:S(2)}, u32[]{:S(2)}) collective-permute-start(bf16[512,768]{1,0:T(8,128)(2,1)} %get-tuple-element.102.refs_0_), channel_id=1, source_target_pairs={{0,2},{1,3},{2,0},{3,1},{4,6},{5,7},{6,4},{7,5},{8,10},{9,11},{10,... | collective-permute-start | bytes 2359304 | tf_op jit(solution)/shard_map/ppermute | solution.py:774
  121.4 85.3 %collective-permute-start.33 = (bf16[512,768]{1,0:T(8,128)(2,1)}, bf16[512,768]{1,0:T(8,128)(2,1)S(1)}, u32[]{:S(2)}, u32[]{:S(2)}) collective-permute-start(bf16[512,768]{1,0:T(8,128)(2,1)} %get-tuple-element.71.ddown.refs_2_), channel_id=1, source_target_pairs={{16,18},{17,19},{18,16},{19,17},{20,22},{21,23},{22,20},{23,21},{2... | collective-permute-start | bytes 2359304 | tf_op jit(solution)/shard_map/ppermute | solution.py:774
  130.2 27.4 %collective-permute-start.10 = (bf16[512,768]{1,0:T(8,128)(2,1)}, bf16[512,768]{1,0:T(8,128)(2,1)S(1)}, u32[]{:S(2)}, u32[]{:S(2)}) collective-permute-start(bf16[512,768]{1,0:T(8,128)(2,1)} %get-tuple-element.80), channel_id=1, source_target_pairs={{16,0},{17,1},{18,2},{19,3},{20,4},{21,5},{22,6},{23,7},{24,8},{25... | collective-permute-start | bytes 2359304 | tf_op jit(solution)/shard_map/ppermute | solution.py:848
  135.9 150.4 %collective-permute-start.22 = (bf16[8,192,768]{2,1,0:T(8,128)(2,1)}, bf16[8,192,768]{2,1,0:T(8,128)(2,1)}, u32[]{:S(2)}, u32[]{:S(2)}) collective-permute-start(bf16[8,192,768]{2,1,0:T(8,128)(2,1)} %get-tuple-element.101), channel_id=1, source_target_pairs={{16,18},{17,19},{18,16},{19,17},{20,22},{21,23},{22,20},{23,21},{2... | collective-permute-start | bytes 7077896 | tf_op jit(solution)/shard_map/ppermute | solution.py:774
  157.6 0.9 copy-start.5
  163.6 50.2 %collective-permute-start.28 = (bf16[512,768]{1,0:T(8,128)(2,1)}, bf16[512,768]{1,0:T(8,128)(2,1)S(1)}, u32[]{:S(2)}, u32[]{:S(2)}) collective-permute-start(bf16[512,768]{1,0:T(8,128)(2,1)} %get-tuple-element.81.ddown.refs_2_), channel_id=1, source_target_pairs={{0,2},{1,3},{2,0},{3,1},{4,6},{5,7},{6,4},{7,5},{8,10},{9,11},{10,... | collective-permute-start | bytes 2359304 | tf_op jit(solution)/shard_map/ppermute | solution.py:774
  203.3 86.5 %collective-permute-start.17 = (bf16[8,192,768]{2,1,0:T(8,128)(2,1)}, bf16[8,192,768]{2,1,0:T(8,128)(2,1)}, u32[]{:S(2)}, u32[]{:S(2)}) collective-permute-start(bf16[8,192,768]{2,1,0:T(8,128)(2,1)} %get-tuple-element.98), channel_id=1, source_target_pairs={{0,2},{1,3},{2,0},{3,1},{4,6},{5,7},{6,4},{7,5},{8,10},{9,11},{10,... | collective-permute-start | bytes 7077896 | tf_op jit(solution)/shard_map/ppermute | solution.py:774
  206.7 0.9 copy-start.15
  206.7 1.1 copy-start.16
  209.1 87.4 %collective-permute-start.34 = (bf16[4,384,768]{2,1,0:T(8,128)(2,1)}, bf16[4,384,768]{2,1,0:T(8,128)(2,1)}, u32[]{:S(2)}, u32[]{:S(2)}) collective-permute-start(bf16[4,384,768]{2,1,0:T(8,128)(2,1)} %get-tuple-element.109), channel_id=1, source_target_pairs={{16,17},{17,16},{18,19},{19,18},{20,21},{21,20},{22,23},{23,22},{2... | collective-permute-start | bytes 7077896 | tf_op jit(solution)/shard_map/ppermute | solution.py:774
  213.8 0.9 copy-start.17
  214.7 68.5 %copy-start.6 = (bf16[512,768]{1,0:T(8,128)(2,1)S(1)}, bf16[512,768]{1,0:T(8,128)(2,1)}, u32[]{:S(2)}) copy-start(bf16[512,768]{1,0:T(8,128)(2,1)} %get-tuple-element.94) | copy-start | bytes 2359300
  214.7 71.6 %copy-start = (bf16[8,192,768]{2,1,0:T(8,128)(2,1)S(1)}, bf16[8,192,768]{2,1,0:T(8,128)(2,1)}, u32[]{:S(2)}) copy-start(bf16[8,192,768]{2,1,0:T(8,128)(2,1)} %get-tuple-element.100) | copy-start | bytes 7077892
  234.3 76.6 %collective-permute-start.29 = (bf16[4,384,768]{2,1,0:T(8,128)(2,1)}, bf16[4,384,768]{2,1,0:T(8,128)(2,1)}, u32[]{:S(2)}, u32[]{:S(2)}) collective-permute-start(bf16[4,384,768]{2,1,0:T(8,128)(2,1)} %get-tuple-element.106), channel_id=1, source_target_pairs={{0,1},{1,0},{2,3},{3,2},{4,5},{5,4},{6,7},{7,6},{8,9},{9,8},{10,11... | collective-permute-start | bytes 7077896 | tf_op jit(solution)/shard_map/ppermute | solution.py:774
  236.5 36.4 %collective-permute-start.11 = (f32[13,768]{1,0:T(8,128)S(1)}, f32[13,768]{1,0:T(8,128)S(1)}, u32[]{:S(2)}, u32[]{:S(2)}) collective-permute-start(f32[13,768]{1,0:T(8,128)S(1)} %pad_maximum_fusion.4), channel_id=1, source_target_pairs={{0,1},{1,0},{2,3},{3,2},{4,5},{5,4},{6,7},{7,6},{8,9},{9,8},{10,11... | collective-permute-start | bytes 119816 | tf_op jit(solution)/shard_map/ppermute | solution.py:774
  272.9 4.2 %collective-permute-start.12 = (f32[13,768]{1,0:T(8,128)S(1)}, f32[13,768]{1,0:T(8,128)S(1)}, u32[]{:S(2)}, u32[]{:S(2)}) collective-permute-start(f32[13,768]{1,0:T(8,128)S(1)} %fusion.31), channel_id=1, source_target_pairs={{0,2},{1,3},{2,0},{3,1},{4,6},{5,7},{6,4},{7,5},{8,10},{9,11},{10,... | collective-permute-start | bytes 119816 | tf_op jit(solution)/shard_map/ppermute | solution.py:774
  277.1 4.2 %collective-permute-start.13 = (f32[13,768]{1,0:T(8,128)S(1)}, f32[13,768]{1,0:T(8,128)S(1)}, u32[]{:S(2)}, u32[]{:S(2)}) collective-permute-start(f32[13,768]{1,0:T(8,128)S(1)} %add.201), channel_id=1, source_target_pairs={{0,4},{1,5},{2,6},{3,7},{4,0},{5,1},{6,2},{7,3},{8,12},{9,13},{10,... | collective-permute-start | bytes 119816 | tf_op jit(solution)/shard_map/ppermute | solution.py:774
  281.2 5.0 %collective-permute-start.14 = (f32[13,768]{1,0:T(8,128)S(1)}, f32[13,768]{1,0:T(8,128)S(1)}, u32[]{:S(2)}, u32[]{:S(2)}) collective-permute-start(f32[13,768]{1,0:T(8,128)S(1)} %add.202), channel_id=1, source_target_pairs={{0,8},{1,9},{2,10},{3,11},{4,12},{5,13},{6,14},{7,15},{8,0},{9,1},... | collective-permute-start | bytes 119816 | tf_op jit(solution)/shard_map/ppermute | solution.py:774
  286.3 15.4 %copy-start.12 = (f32[13,768]{1,0:T(8,128)}, f32[13,768]{1,0:T(8,128)S(1)}, u32[]{:S(2)}) copy-start(f32[13,768]{1,0:T(8,128)S(1)} %add.203) | copy-start | bytes 119812
  286.3 3.5 copy-start.1
  289.1 25.7 %collective-permute-start.23 = (bf16[4,192,768]{2,1,0:T(8,128)(2,1)}, bf16[4,192,768]{2,1,0:T(8,128)(2,1)S(1)}, u32[]{:S(2)}, u32[]{:S(2)}) collective-permute-start(bf16[4,192,768]{2,1,0:T(8,128)(2,1)} %add_convert_fusion), channel_id=1, source_target_pairs={{16,17},{17,16},{18,19},{19,18},{20,21},{21,20},{22,23},{23,22},{2... | collective-permute-start | bytes 3538952 | tf_op jit(solution)/shard_map/ppermute | solution.py:774
  289.8 6.7 %copy-start.2 = (bf16[4,384,768]{2,1,0:T(8,128)(2,1)S(1)}, bf16[4,384,768]{2,1,0:T(8,128)(2,1)}, u32[]{:S(2)}) copy-start(bf16[4,384,768]{2,1,0:T(8,128)(2,1)} %get-tuple-element.108) | copy-start | bytes 7077892
  292.6 28.6 %collective-permute-start.18 = (bf16[4,192,768]{2,1,0:T(8,128)(2,1)}, bf16[4,192,768]{2,1,0:T(8,128)(2,1)}, u32[]{:S(2)}, u32[]{:S(2)}) collective-permute-start(bf16[4,192,768]{2,1,0:T(8,128)(2,1)} %add_convert_fusion.1), channel_id=1, source_target_pairs={{0,1},{1,0},{2,3},{3,2},{4,5},{5,4},{6,7},{7,6},{8,9},{9,8},{10,11... | collective-permute-start | bytes 3538952 | tf_op jit(solution)/shard_map/ppermute | solution.py:774
  295.2 9.6 %collective-permute-start.15 = (f32[128]{0:T(128)}, f32[128]{0:T(128)S(1)}, u32[]{:S(2)}, u32[]{:S(2)}) collective-permute-start(f32[128]{0:T(128)} %slice_bitcast_fusion.3), channel_id=1, source_target_pairs={{16,0},{17,1},{18,2},{19,3},{20,4},{21,5},{22,6},{23,7},{24,8},{25... | collective-permute-start | bytes 1544 | tf_op jit(solution)/shard_map/ppermute | solution.py:848
  299.5 19.4 %collective-permute-start.37 = (bf16[384,768]{1,0:T(8,128)(2,1)}, bf16[384,768]{1,0:T(8,128)(2,1)}, u32[]{:S(2)}, u32[]{:S(2)}) collective-permute-start(bf16[384,768]{1,0:T(8,128)(2,1)} %get-tuple-element.122), channel_id=1, source_target_pairs={{16,28},{17,29},{18,30},{19,31},{20,24},{21,25},{22,26},{23,27},{2... | collective-permute-start | bytes 1769480 | tf_op jit(solution)/shard_map/ppermute | solution.py:774
  304.8 9.3 %collective-permute-start.16 = (bf16[2,128,768]{2,1,0:T(8,128)(2,1)}, bf16[2,128,768]{2,1,0:T(8,128)(2,1)S(1)}, u32[]{:S(2)}, u32[]{:S(2)}) collective-permute-start(bf16[2,128,768]{2,1,0:T(8,128)(2,1)} %slice.339), channel_id=1, source_target_pairs={{0,16},{1,17},{2,18},{3,19},{4,20},{5,21},{6,22},{7,23},{8,24},{9,... | collective-permute-start | bytes 1179656 | tf_op jit(solution)/shard_map/ppermute | solution.py:977
  310.9 20.1 %collective-permute-start.36 = (bf16[384,768]{1,0:T(8,128)(2,1)}, bf16[384,768]{1,0:T(8,128)(2,1)S(1)}, u32[]{:S(2)}, u32[]{:S(2)}) collective-permute-start(bf16[384,768]{1,0:T(8,128)(2,1)} %get-tuple-element.123), channel_id=1, source_target_pairs={{16,24},{17,25},{18,26},{19,27},{20,28},{21,29},{22,30},{23,31},{2... | collective-permute-start | bytes 1769480 | tf_op jit(solution)/shard_map/ppermute | solution.py:774
  311.5 2.5 copy-start.9
  311.6 13.4 %copy-start.7 = (bf16[512,768]{1,0:T(8,128)(2,1)S(1)}, bf16[512,768]{1,0:T(8,128)(2,1)}, u32[]{:S(2)}) copy-start(bf16[512,768]{1,0:T(8,128)(2,1)} %get-tuple-element.94) | copy-start | bytes 2359300
  314.1 18.3 %collective-permute-start.35 = (bf16[384,768]{1,0:T(8,128)(2,1)S(1)}, bf16[384,768]{1,0:T(8,128)(2,1)S(1)}, u32[]{:S(2)}, u32[]{:S(2)}) collective-permute-start(bf16[384,768]{1,0:T(8,128)(2,1)S(1)} %copy-done.9), channel_id=1, source_target_pairs={{16,20},{17,21},{18,22},{19,23},{20,16},{21,17},{22,18},{23,19},{2... | collective-permute-start | bytes 1769480 | tf_op jit(solution)/shard_map/ppermute | solution.py:774
  314.8 13.4 %copy-start.3 = (bf16[4,192,768]{2,1,0:T(8,128)(2,1)}, bf16[4,192,768]{2,1,0:T(8,128)(2,1)S(1)}, u32[]{:S(2)}) copy-start(bf16[4,192,768]{2,1,0:T(8,128)(2,1)S(1)} %collective-permute-done.23) | copy-start | bytes 3538948
  314.8 20.0 %collective-permute-start.32 = (bf16[384,768]{1,0:T(8,128)(2,1)S(1)}, bf16[384,768]{1,0:T(8,128)(2,1)S(1)}, u32[]{:S(2)}, u32[]{:S(2)}) collective-permute-start(bf16[384,768]{1,0:T(8,128)(2,1)S(1)} %get-tuple-element.119), channel_id=1, source_target_pairs={{0,12},{1,13},{2,14},{3,15},{4,8},{5,9},{6,10},{7,11},{8,4},{9,5},... | collective-permute-start | bytes 1769480 | tf_op jit(solution)/shard_map/ppermute | solution.py:774
  318.9 37.5 %collective-permute-start.31 = (bf16[384,768]{1,0:T(8,128)(2,1)S(1)}, bf16[384,768]{1,0:T(8,128)(2,1)S(1)}, u32[]{:S(2)}, u32[]{:S(2)}) collective-permute-start(bf16[384,768]{1,0:T(8,128)(2,1)S(1)} %get-tuple-element.120), channel_id=1, source_target_pairs={{0,8},{1,9},{2,10},{3,11},{4,12},{5,13},{6,14},{7,15},{8,0},{9,1},... | collective-permute-start | bytes 1769480 | tf_op jit(solution)/shard_map/ppermute | solution.py:774
  321.2 40.1 %collective-permute-start.30 = (bf16[384,768]{1,0:T(8,128)(2,1)S(1)}, bf16[384,768]{1,0:T(8,128)(2,1)S(1)}, u32[]{:S(2)}, u32[]{:S(2)}) collective-permute-start(bf16[384,768]{1,0:T(8,128)(2,1)S(1)} %get-tuple-element.118), channel_id=1, source_target_pairs={{0,4},{1,5},{2,6},{3,7},{4,0},{5,1},{6,2},{7,3},{8,12},{9,13},{10,... | collective-permute-start | bytes 1769480 | tf_op jit(solution)/shard_map/ppermute | solution.py:774
  331.0 35.7 %collective-permute-start.26 = (bf16[192,768]{1,0:T(8,128)(2,1)S(1)}, bf16[192,768]{1,0:T(8,128)(2,1)}, u32[]{:S(2)}, u32[]{:S(2)}) collective-permute-start(bf16[192,768]{1,0:T(8,128)(2,1)S(1)} %get-tuple-element.116), channel_id=1, source_target_pairs={{16,28},{17,29},{18,30},{19,31},{20,24},{21,25},{22,26},{23,27},{2... | collective-permute-start | bytes 884744 | tf_op jit(solution)/shard_map/ppermute | solution.py:774
  332.3 42.7 %collective-permute-start.25 = (bf16[192,768]{1,0:T(8,128)(2,1)}, bf16[192,768]{1,0:T(8,128)(2,1)}, u32[]{:S(2)}, u32[]{:S(2)}) collective-permute-start(bf16[192,768]{1,0:T(8,128)(2,1)} %get-tuple-element.117), channel_id=1, source_target_pairs={{16,24},{17,25},{18,26},{19,27},{20,28},{21,29},{22,30},{23,31},{2... | collective-permute-start | bytes 884744 | tf_op jit(solution)/shard_map/ppermute | solution.py:774
  334.7 40.8 %collective-permute-start.24 = (bf16[192,768]{1,0:T(8,128)(2,1)}, bf16[192,768]{1,0:T(8,128)(2,1)}, u32[]{:S(2)}, u32[]{:S(2)}) collective-permute-start(bf16[192,768]{1,0:T(8,128)(2,1)} %get-tuple-element.115), channel_id=1, source_target_pairs={{16,20},{17,21},{18,22},{19,23},{20,16},{21,17},{22,18},{23,19},{2... | collective-permute-start | bytes 884744 | tf_op jit(solution)/shard_map/ppermute | solution.py:774
  356.3 19.2 %collective-permute-start.21 = (bf16[192,768]{1,0:T(8,128)(2,1)}, bf16[192,768]{1,0:T(8,128)(2,1)}, u32[]{:S(2)}, u32[]{:S(2)}) collective-permute-start(bf16[192,768]{1,0:T(8,128)(2,1)} %get-tuple-element.113), channel_id=1, source_target_pairs={{0,12},{1,13},{2,14},{3,15},{4,8},{5,9},{6,10},{7,11},{8,4},{9,5},... | collective-permute-start | bytes 884744 | tf_op jit(solution)/shard_map/ppermute | solution.py:774
  361.3 21.4 %collective-permute-start.20 = (bf16[192,768]{1,0:T(8,128)(2,1)}, bf16[192,768]{1,0:T(8,128)(2,1)}, u32[]{:S(2)}, u32[]{:S(2)}) collective-permute-start(bf16[192,768]{1,0:T(8,128)(2,1)} %get-tuple-element.114), channel_id=1, source_target_pairs={{0,8},{1,9},{2,10},{3,11},{4,12},{5,13},{6,14},{7,15},{8,0},{9,1},... | collective-permute-start | bytes 884744 | tf_op jit(solution)/shard_map/ppermute | solution.py:774
  366.6 16.1 %collective-permute-start.19 = (bf16[192,768]{1,0:T(8,128)(2,1)}, bf16[192,768]{1,0:T(8,128)(2,1)}, u32[]{:S(2)}, u32[]{:S(2)}) collective-permute-start(bf16[192,768]{1,0:T(8,128)(2,1)} %get-tuple-element.112), channel_id=1, source_target_pairs={{0,4},{1,5},{2,6},{3,7},{4,0},{5,1},{6,2},{7,3},{8,12},{9,13},{10,... | collective-permute-start | bytes 884744 | tf_op jit(solution)/shard_map/ppermute | solution.py:774
  375.0 11.5 %collective-permute-start.38 = (f32[48,4,384]{2,1,0:T(4,128)}, f32[48,4,384]{2,1,0:T(4,128)S(1)}, u32[]{:S(2)}, u32[]{:S(2)}) collective-permute-start(f32[48,4,384]{2,1,0:T(4,128)} %reshape.205), channel_id=1, source_target_pairs={{0,2},{1,3},{2,0},{3,1},{4,6},{5,7},{6,4},{7,5},{8,10},{9,11},{10,... | collective-permute-start | bytes 884744 | tf_op jit(solution)/shard_map/ppermute | solution.py:774
  385.0 1.5 copy-start.4
where the time goes:
time: 395 us; the launch traced here: 389 us
  Pallas kernels  158 us (40%)
  waiting for transfers between devices  99.5 us (25%)
  starting transfers between devices  72.2 us (18%)
  local copies, waits for them, and re-layouts  29.8 us (8%)
  other arithmetic  27.4 us (7%)
    pallas_call x15, Pallas kernels, call(): pl.pallas_call(kernel, out_shape=[sd(*o) for o in outs], in_specs=in_spec...  158 us
    ppermute x32, waiting for transfers between devices, swap(): return lax.ppermute(block, AXES, route)  78.9 us
    ppermute x32, starting transfers between devices, swap(): return lax.ppermute(block, AXES, route)  58.5 us
    ppermute x6, waiting for transfers between devices, relay(): lax.ppermute(block, 'section', [(0, 1)] if distance > 0 else [(1, 0)])  20.6 us
    convert_element_type x6, other arithmetic, low(): return v.astype(BF)  16 us
    unnamed x43, local copies, waits for them, and re-layouts  9.02 us
    ppermute x6, starting transfers between devices, relay(): lax.ppermute(block, 'section', [(0, 1)] if distance > 0 else [(1, 0)])  8.84 us
  transfers between devices with their start and end apart: 39, of which 14 were waited for; matrix products, arithmetic and copies ran while one was open for 13% of the time, Pallas kernels for 21%

commit v1 on v0

--- a/solution.py
+++ b/solution.py
@@ -326,6 +326,8 @@
         token = lax.broadcasted_iota(jnp.int32, (block, 1), 0) + (i % per_crop) * block
         part = jnp.sum(jnp.where(token < lens[c], f, 0.0), axis=0, keepdims=True)
         pool_ref[c : c + 1, :] += part / lens[c].astype(F32)
+    pooled = pool_ref[:crops]
+    pool_ref[crops : 2 * crops] = pooled * lax.rsqrt(jnp.sum(pooled * pooled, axis=-1, keepdims=True) + 1e-6)
     if save:
         copies.send(n2, n2_o)
         copies.send(r2, r2_o)
@@ -709,7 +711,11 @@
     def run():
         n_x = len(x_kinds) + 1
         x_refs = refs[:n_x]
-        ctx_h, datt_h, dqkv_h, out_a, out_b, x, ctx, datt, dqkv, gqkv, gout, sems = refs[n_x:]
+        if fast:
+            vec_a, vec_b, vec_c, bup, lost, *refs_ = refs[n_x:]
+            ctx_h, datt_h, dqkv_h, out_a, out_b, x, ctx, datt, dqkv, gqkv, gout, tail, sems = refs_
+        else:
+            ctx_h, datt_h, dqkv_h, out_a, out_b, x, ctx, datt, dqkv, gqkv, gout, sems = refs[n_x:]
         copies = Copies(sems)
         got = [copies.fetch(ctx_h, ctx), copies.fetch(datt_h, datt)]
         got_x = fetch_rows(copies, x_refs, x_kinds, x)
@@ -727,6 +733,19 @@
             copies.send(gout, out_b)
         else:
             z, xx, y = place_bits()
+            picked = [vec_c[1:2], vec_b[2:3], vec_b[1:2], vec_a[2:3], vec_a[1:2], vec_b[0:1], vec_a[0:1], vec_c[0:1]]
+            small = jnp.concatenate([p[...] for p in picked], axis=0)
+            row = lax.broadcasted_iota(jnp.int32, (8, D), 0)
+            lane = lax.broadcasted_iota(jnp.int32, (8, D), 1) - 3 * ((z * 2 + xx) * 2 + y)
+            terms = [jnp.broadcast_to(t.astype(F32)[0:1, 0:1], (8, D)) for t in split3(lost[...])]
+            lost_row = sum(jnp.where(lane == i, t, 0.0) for i, t in enumerate(terms))
+            for j in range(16):
+                jx, jy, jz = j // 8, j // 4 % 2, j % 4
+                owner = (jnp.bitwise_xor(z, jz) * 2 + jnp.bitwise_xor(xx, jx)) * 2 + jnp.bitwise_xor(y, jy)
+                head = pltpu.roll(small, D - 48 * owner, 1)
+                ups = pltpu.roll(bup[...], FF - 192 * owner, 1)[:, :D]
+                other = jnp.where(row == 0, ups, jnp.where(row == 1, lost_row, 0.0))
+                tail[j] = jnp.concatenate([head, other], axis=0).astype(BF)
             for j in range(15, -1, -1):
                 jx, jy, jz = j // 8, j // 4 % 2, j % 4
                 owner = (jnp.bitwise_xor(z, jz) * 2 + jnp.bitwise_xor(xx, jx)) * 2 + jnp.bitwise_xor(y, jy)
@@ -735,25 +754,29 @@
                 for t in range(3):
                     copies.send(gqkv.at[at, slice(D * t, D * (t + 1))], out.at[48 * t : 48 * (t + 1), :])
                 copies.send(gout.at[at, :], out.at[144:192, :])
+                copies.send(tail.at[j], out.at[192:208, :])
         copies.drain()
 
     only_on(active, run)
 
 
-def attention_weights(active, halves, whole, ctx, datt, dqkv):
+def attention_weights(active, halves, whole, ctx, datt, dqkv, small):
     rows = ctx.shape[0]
     fast = fast_mesh()
     x_kinds = ("halves", "whole")
-    outs = [((8, 192, D), BF)] * 2 if fast else [((D, 3 * D), BF), ((D, D), BF)]
-    ins = [*halves, whole, ctx, datt, dqkv]
+    outs = [((8, 208, D), BF)] * 2 if fast else [((D, 3 * D), BF), ((D, D), BF)]
+    ins = [*halves, whole, *(small if fast else ()), ctx, datt, dqkv]
+    in_specs = [ANY] * 3 + [VMEM] * (5 if fast else 0) + [ANY] * 3
     return call(
         functools.partial(attention_weights_kernel, rows, active, fast, x_kinds),
         "attention_weights",
         outs,
         [ANY] * 2,
         ins,
-        [ANY] * len(ins),
-        [((rows, D), BF)] * 3 + [((rows, 3 * D), BF), ((D, 3 * D), BF), ((D, D), BF)],
+        in_specs,
+        [((rows, D), BF)] * 3
+        + [((rows, 3 * D), BF), ((D, 3 * D), BF), ((D, D), BF)]
+        + ([((16, 16, D), BF)] if fast else []),
         rows * 8 * D * D,
         12000000,
     )
@@ -786,30 +809,149 @@
     return out
 
 
-def low(v):
-    return v.astype(BF)
-
-
-def wide(*terms):
-    total = terms[0].astype(F32)
-    for t in terms[1:]:
-        total = total + t.astype(F32)
-    return total
-
-
-def attention_sum(keep, send, section):
-    first = swap(send, section, 1, 0)
-    second = swap(low(wide(keep[4:], first[4:])), section, 0, 1)
-    parts = [wide(keep[k], first[k], second[k]) for k in range(4)]
-    others = [swap(low(parts[k]), section, 2 * k, 0) for k in range(1, 4)]
-    return wide(parts[0], *others)
-
-
-def ffn_sum(keep, send, section):
-    first = swap(send, section, 0, 1)
-    parts = [wide(keep[k], first[k]) for k in range(4)]
-    others = [swap(low(parts[k]), section, 2 * k, 0) for k in range(1, 4)]
-    return wide(parts[0], *others)
+def add_rows(pieces, dst, at, count):
+    def step(i, carry):
+        here = pl.ds(pl.multiple_of(i * 16, 16), 16)
+        total = pieces[0][here, :].astype(F32)
+        for p in pieces[1:]:
+            total = total + p[here, :].astype(F32)
+        dst[pl.ds(pl.multiple_of(at + i * 16, 16), 16), :] = total.astype(dst.dtype)
+        return carry
+
+    lax.fori_loop(0, count // 16, step, 0, unroll=2 if count % 32 == 0 else 1)
+
+
+def partial_kernel(active, slots, joined, n_in, rows, *refs):
+    def run():
+        ins, outs = refs[:n_in], refs[n_in : n_in + (1 if joined else len(slots))]
+        held, made, sems = refs[-3:]
+        copies = Copies(sems)
+        got = [[copies.fetch(r.at[k], held.at[i, t]) for t, r in enumerate(ins)] for i, k in enumerate(slots)]
+        for i in range(len(slots)):
+            for cp in got[i]:
+                cp.wait()
+            add_rows([held.at[i, t] for t in range(n_in)], made.at[i], 0, rows)
+            copies.send(made.at[i], outs[0].at[i] if joined else outs[i])
+        copies.drain()
+
+    only_on(active, run)
+
+
+def partial_sums(active, slots, joined, ins):
+    shape = ins[0].shape[1:]
+    n = len(slots)
+    outs = [((n, *shape), BF)] if joined else [(shape, BF)] * n
+    made = call(
+        functools.partial(partial_kernel, active, slots, joined, len(ins), shape[0]),
+        "partial_sums",
+        outs,
+        [ANY] * len(outs),
+        list(ins),
+        [ANY] * len(ins),
+        [((n, len(ins), *shape), BF), ((n, *shape), BF)],
+        n * len(ins) * shape[0] * shape[1],
+        2 * n * (len(ins) + 1) * shape[0] * shape[1],
+    )
+    return made[0] if joined else made
+
+
+def fetch_terms(copies, refs, n_slotted, held):
+    half = len(refs) // 2
+    got = []
+    for t in range(half):
+        pair = (refs[t], refs[half + t])
+        if t < n_slotted:
+            pair = tuple(r.at[0] for r in pair)
+        got.append(copies.pick(pair, held.at[t]))
+    for cp in got:
+        cp.wait()
+    return [held.at[t] for t in range(half)]
+
+
+def attention_total_kernel(*refs):
+    qkv_o, out_o, bias_o, gain_o, query_o, up_o, loss_o, held, total, sems = refs[12:]
+    terms = fetch_terms(Copies(sems), refs[:12], 3, held)
+    add_rows(terms, total, 0, 208)
+    for t in range(3):
+        qkv_o[:, D * t : D * (t + 1)] = total[48 * t : 48 * (t + 1), :]
+    out_o[...] = total[144:192, :]
+    bias_o[...] = total[192:197, :48]
+    gain_o[...] = total[197:199, :48]
+    query_o[...] = total[199:200, :48]
+    up_o[...] = total[200:201, :192]
+    loss_o[...] = jnp.broadcast_to(jnp.sum(total[201:202, :], axis=-1, keepdims=True), loss_o.shape)
+
+
+def ffn_total_kernel(*refs):
+    down_o, own_o, peer_o, held, total, sems = refs[10:]
+    terms = fetch_terms(Copies(sems), refs[:10], 2, held)
+    add_rows(terms, total, 0, 384)
+    own_o[...] = total[0:96, :]
+    peer_o[...] = total[96:192, :].astype(BF)
+    down_o[...] = total[192:384, :]
+
+
+def up_total_kernel(own, peer, up_o, sems):
+    x = lax.axis_index("dp") % 2
+    for c in range(2):
+        for k in range(2):
+            cols = slice(384 * k, 384 * (k + 1))
+            at = 768 * (2 * c + k)
+            up_o[:, pl.ds(pl.multiple_of(at + 384 * x, 128), 384)] = own[48 * c : 48 * (c + 1), cols]
+            up_o[:, pl.ds(pl.multiple_of(at + 384 * (1 - x), 128), 384)] = peer[48 * c : 48 * (c + 1), cols].astype(F32)
+
+
+def totals(kernel, name, ins, rows, outs, in_spec=ANY):
+    terms = len(ins) // 2
+    scratch = [((terms, rows, D), BF), ((rows, D), F32)] if rows else []
+    return call(kernel, name, outs, [VMEM] * len(outs), ins, [in_spec] * len(ins), scratch, 1000000, 4000000)
+
+
+def after(value, *others):
+    return lax.optimization_barrier((value, others))[0]
+
+
+def chip_sums(attention, ffn, last):
+    (ka0, sa0), (ka1, sa1) = attention
+    (kf0, sf0), (kf1, sf1) = ffn
+    a1 = swap(sa1, last, 1, 0)
+    f1 = swap(sf1, last, 0, 1)
+    f0 = swap(sf0, 0, 0, 1)
+    a0 = swap(sa0, 0, 1, 0)
+    distances = (1, 2, 3)
+
+    def over_z(parts, section):
+        return [swap(p, section, 2 * k, 0) for k, p in zip(distances, parts)]
+
+    s1 = partial_sums(last, (4, 5, 6, 7), True, [ka1, after(a1, ka0)])
+    b1 = swap(s1, last, 0, 1)
+    p1 = partial_sums(last, distances, False, [kf1, after(f1, s1)])
+    g1 = over_z(p1, last)
+    p0 = partial_sums(0, distances, False, [kf0, after(f0, *p1)])
+    g0 = over_z(p0, 0)
+    s0 = partial_sums(0, (4, 5, 6, 7), True, [ka0, after(a0, *p0)])
+    b0 = swap(s0, 0, 0, 1)
+    q1 = partial_sums(last, distances, False, [ka1, a1, after(b1, s0)])
+    h1 = over_z(q1, last)
+    q0 = partial_sums(0, distances, False, [ka0, a0, after(b0, *q1)])
+    h0 = over_z(q0, 0)
+    down, own, peer = totals(
+        ffn_total_kernel,
+        "ffn_total",
+        [kf0, f0, *g0, kf1, after(f1, *q0), *g1],
+        384,
+        [((192, D), F32), ((96, D), F32), ((96, D), BF)],
+    )
+    peer = swap(peer, None, 1, 0)
+    qkv, out, bias, gain, query, up_bias, loss = totals(
+        attention_total_kernel,
+        "attention_total",
+        [ka0, a0, b0, *h0, ka1, after(a1, down), b1, *h1],
+        208,
+        [((48, 3 * D), F32), ((48, D), F32), ((5, 48), F32), ((2, 48), F32), ((1, 48), F32), ((1, 192), F32), ((8, 128), F32)],
+    )
+    (up,) = totals(up_total_kernel, "up_total", [own, peer], 0, [((48, FF), F32)], VMEM)
+    return qkv, out, up, down, bias, gain, up_bias, query, loss
 
 
 def body(
@@ -871,8 +1013,7 @@
     query_middle, key_pooled = forward(rows, None, False, query_halves, key_middle, [query_encoder, key_encoder])
     query_middle = relay(query_middle, 1)
 
-    every_key = key_pooled[:crops]
-    every_key = every_key * lax.rsqrt(jnp.sum(every_key * every_key, axis=-1, keepdims=True) + 1e-6)
+    every_key = key_pooled[crops : 2 * crops]
     near_flips = [(0, 1), (1, 0), (1, 1)]
     if fast:
         every_key = jnp.concatenate([every_key] + [swap(every_key, None, *f) for f in near_flips], axis=0)
@@ -919,62 +1060,49 @@
     def attention_part(active, datt, dsum1):
         return attention_backward(active, datt, dsum1, qkv, prob, query_weights[1], query_weights[0])
 
-    def attention_grads(active, datt, dqkv):
-        return attention_weights(active, query_halves, query_middle, ctx, datt, dqkv)
-
-    def small_rows(vec_a, vec_b, vec_c, grad_bup):
+    def attention_grads(active, datt, dqkv, small):
+        return attention_weights(active, query_halves, query_middle, ctx, datt, dqkv, small)
+
+    def small_rows(vec_a, vec_b, vec_c, grad_bup, lost):
         picked = [vec_c[1:2], vec_b[2:3], vec_b[1:2], vec_a[2:3], vec_a[1:2], vec_b[0:1], vec_a[0:1], vec_c[0:1]]
-        return jnp.concatenate(picked + [grad_bup[0:1].reshape(FF // D, D)], axis=0)
+        lost_row = jnp.concatenate([lost[0:1]] * (D // 128), axis=1)
+        return jnp.concatenate(picked + [grad_bup[0:1].reshape(FF // D, D), lost_row], axis=0)
 
     ddown, ddown_peer, dup, datt, dsum1, vec_a, vec_b, grad_bup = ffn_part(last, True, pooled_grad)
     dmiddle, vec_c, dqkv = attention_part(last, datt, dsum1)
-    small_last = small_rows(vec_a, vec_b, vec_c, grad_bup)
+    small_last = (vec_a, vec_b, vec_c, grad_bup, lost)
     dmiddle = relay(dmiddle, -1)
-    attention_last = attention_grads(last, datt, dqkv)
+    attention_last = attention_grads(last, datt, dqkv, small_last)
     ffn_last = ffn_grads(last, ddown, ddown_peer, dup)
 
-    ddown, ddown_peer, dup, datt, dsum1, vec_a, vec_b, grad_bup = ffn_part(0, False, dmiddle)
+    ddown, ddown_peer, dup, datt, dsum1, vec_a, vec_b, grad_bup = ffn_part(0, False, after(dmiddle, *ffn_last))
     ffn_first = ffn_grads(0, ddown, ddown_peer, dup)
-    dx, vec_c, dqkv = attention_part(0, datt, dsum1)
-    small_first = small_rows(vec_a, vec_b, vec_c, grad_bup)
-    attention_first = attention_grads(0, datt, dqkv)
+    dx, vec_c, dqkv = attention_part(0, after(datt, *ffn_first), dsum1)
+    small_first = (vec_a, vec_b, vec_c, grad_bup, jnp.zeros_like(lost))
+    attention_first = attention_grads(0, datt, dqkv, small_first)
 
     if fast:
-        attention_total = [attention_sum(*attention_first, 0), attention_sum(*attention_last, last)]
-        ffn_total = [ffn_sum(ffn_first[1], ffn_first[0], 0), ffn_sum(ffn_last[1], ffn_last[0], last)]
-        attention_total = jnp.where(on_first, *attention_total)
-        ffn_total = jnp.where(on_first, *ffn_total)
-        grad_qkv = jnp.concatenate([attention_total[48 * t : 48 * (t + 1)] for t in range(3)], axis=1)
-        grad_out = attention_total[144:]
-        grad_down = ffn_total[192:]
-
-        def joined(rows96):
-            return jnp.concatenate([rows96[:48], rows96[48:96]], axis=1).reshape(48, 4, 384)
-
-        own = joined(ffn_total[:96])
-        peer = swap(joined(ffn_total[96:192]), None, 1, 0)
-        even = dp % 2 == 0
-        grad_up = jnp.stack([jnp.where(even, own, peer), jnp.where(even, peer, own)], axis=2).reshape(48, FF)
+        summed = chip_sums((attention_first, attention_last), (ffn_first[::-1], ffn_last[::-1]), last)
+        grad_qkv, grad_out, grad_up, grad_down, bias, gain, up_part, query_part, loss_row = summed
+        loss_row = loss_row[0]
     else:
-        totals = [
+        grad_up, grad_down, grad_qkv, grad_out = [
             lax.psum_scatter(jnp.where(on_first, a, b).astype(F32), ("dp", "rep"), scatter_dimension=0, tiled=True)
             for a, b in zip([*ffn_first, *attention_first], [*ffn_last, *attention_last])
         ]
-        grad_up, grad_down, grad_qkv, grad_out = totals
-
-    small = jnp.where(on_first, small_first, small_last)
-    loss_row = jnp.where(on_first, 0.0, jnp.concatenate([lost[0:1]] * (D // 128), axis=1))
-    small = jnp.concatenate([small, loss_row], axis=0)
-    for flip in flips():
-        small = small + swap(small, None, *flip)
-    loss_value = jnp.where(on_first, relay(small[12, :128], -1), small[12, :128])[:1]
-    width = D // (dps * reps)
-    mine = lax.dynamic_slice(small[:8], (0, place * width), (8, width))
-    up_part = lax.dynamic_slice(small[8:12].reshape(FF), (place * (FF // (dps * reps)),), (FF // (dps * reps),))
+        small = jnp.where(on_first, small_rows(*small_first), small_rows(*small_last))
+        for flip in flips():
+            small = small + swap(small, None, *flip)
+        width, up_width = D // (dps * reps), FF // (dps * reps)
+        mine = lax.dynamic_slice(small[:8], (0, place * width), (8, width))
+        bias, gain, query_part = mine[:5], mine[5:7], mine[7:]
+        up_part = lax.dynamic_slice(small[8:12].reshape(1, FF), (0, place * up_width), (1, up_width))
+        loss_row = small[12, :128]
+    loss_value = jnp.where(on_first, relay(loss_row, -1), loss_row)[:1]
 
     dx = dx.reshape(crops, SLOTS, D)
     half = SLOTS // sections
-    crops_grad = jnp.where(on_first, dx[:, :half], lax.ppermute(dx[:, half:], "section", [(0, 1)])).astype(F32)
+    crops_grad = jnp.where(on_first, dx[:, :half], relay(after(dx[:, half:], grad_down), 1)).astype(F32)
     return (
         loss_value,
         crops_grad,
@@ -982,10 +1110,10 @@
         grad_out[None],
         grad_up[None],
         grad_down[None],
-        mine[None, :5],
-        mine[None, 5:7],
-        up_part[None],
-        mine[None, 7],
+        bias[None],
+        gain[None],
+        up_part,
+        query_part,
     )
 
 

time: 395 us -> 365 us (0.924)
  the two profiles are of different devices: /device:TPU:0 before, /device:TPU:9 now
where the time goes in v1:
time: 365 us; the launch traced here: 360 us
  Pallas kernels  180 us (49%)
  starting transfers between devices  98.8 us (27%)
  waiting for transfers between devices  63.2 us (17%)
  local copies, waits for them, and re-layouts  13.7 us (4%)
    pallas_call x24, Pallas kernels, call(): pl.pallas_call(kernel, out_shape=[sd(*o) for o in outs], in_specs=in_spec...  180 us
    ppermute x28, waiting for transfers between devices, swap(): return lax.ppermute(block, AXES, route)  62.1 us
    ppermute x28, starting transfers between devices, swap(): return lax.ppermute(block, AXES, route)  50.1 us
    ppermute x7, starting transfers between devices, relay(): lax.ppermute(block, 'section', [(0, 1)] if distance > 0 else [(1, 0)])  48.6 us
    unnamed x47, local copies, waits for them, and re-layouts  10.5 us
  transfers between devices with their start and end apart: 35, of which 12 were waited for; matrix products, arithmetic and copies ran while one was open for 2% of the time, Pallas kernels for 33%

profile of v1, /device:TPU:9, one launch (start us, length us, event | category | flops | bytes accessed | tf_op | source)
XLA Modules:
  0.0 359.9 jit_solution(18379813756396276220)
XLA Ops:
  0.6 2.6 collective-permute-start.1
  3.3 9.0 %queue_norm.1.inv = f32[8,4096]{1,0:T(8,128)} custom-call(bf16[4096,768]{1,0:T(8,128)(2,1)} %queue.1), custom_call_target="tpu_custom_call" | custom-call | flops 25165824 | bytes 6291456 | tf_op jit(solution)/shard_map/queue_norm/pallas_call | solution.py:125
  13.0 2.6 layer_forward.3
  15.6 1.3 collective-permute-start.2
  16.9 14.0 %collective-permute-start = (bf16[2,128,768]{2,1,0:T(8,128)(2,1)S(1)}, bf16[2,128,768]{2,1,0:T(8,128)(2,1)S(1)}, u32[]{:S(2)}, u32[]{:S(2)}) collective-permute-start(bf16[2,128,768]{2,1,0:T(8,128)(2,1)S(1)} %copy-done.11), channel_id=1, source_target_pairs={{16,0},{17,1},{18,2},{19,3},{20,4},{21,5},{22,6},{23,7},{24,8},{25... | collective-permute-start | bytes 1179656 | tf_op jit(solution)/shard_map/ppermute | solution.py:990
  30.9 1.1 collective-permute-done.refs_3_.refs_2_.refs_1_
  33.0 21.4 %layer_forward.4 = (bf16[512,768]{1,0:T(8,128)(2,1)}, f32[8,768]{1,0:T(8,128)}) custom-call(s32[2]{0:T(128)} %lens.3, s32[2]{0:T(128)} %refs_1_.4, bf16[2,128,768]{2,1,0:T(8,128)(2,1)} %refs_0_.9, bf16[2,128,768]{2,1,0:T(8,128)(2,1)} %copy-done.12, bf16[512,768]{1,0:T(8,128)(2,1)} %copy-done.6, bf16[768,2304]{1,0:T(8,128)(2,1)} %bitcast.38, ...), custom_call_target="tpu_custom_call" | custom-call | flops 7680000000 | bytes 16000000 | tf_op jit(solution)/shard_map/layer_forward/pallas_call | solution.py:125
  54.4 1.3 collective-permute-start.3
  56.4 2.2 collective-permute-start.6
  59.8 1.6 collective-permute-done.5
  62.5 35.1 %layer_forward.5 = (bf16[512,768]{1,0:T(8,128)(2,1)}, f32[8,768]{1,0:T(8,128)}, bf16[512,2304]{1,0:T(8,128)(2,1)}, bf16[12,512,256]{2,1,0:T(8,128)(2,1)}, bf16[5...) custom-call(s32[2]{0:T(128)} %lens.3, ...), custom_call_target="tpu_custom_call" | custom-call | flops 7680000000 | bytes 31000000 | tf_op jit(solution)/shard_map/layer_forward/pallas_call | solution.py:125
  97.7 1.4 collective-permute-start.9
  99.0 1.1 collective-permute-start.8
  100.1 1.1 collective-permute-start.7
  101.2 1.2 collective-permute-start.11
  104.2 8.0 %contrast.1 = (f32[8,768]{1,0:T(8,128)}, f32[8,128]{1,0:T(8,128)}) custom-call(f32[8,768]{1,0:T(8,128)} %get-tuple-element.98.pooled, f32[8,768]{1,0:T(8,128)} %concatenate.11.matched, bf16[4096,768]{1,0:T(8,128)(2,1)} %queue.1, f32[8,4096]{1,0:T(8,128)} %queue_norm.1.inv), custom_call_target="tpu_custom_call" | custom-call | flops 100663296 | bytes 6291456 | tf_op jit(solution)/shard_map/contrast/pallas_call | solution.py:125
  112.3 4.7 %second_norm_backward.2 = (bf16[512,768]{1,0:T(8,128)(2,1)}, f32[512,768]{1,0:T(8,128)}, f32[8,768]{1,0:T(8,128)}) custom-call(s32[2]{0:T(128)} %lens.3, f32[8,768]{1,0:T(8,128)} %get-tuple-element.101.dy, bf16[512,768]{1,0:T(8,128)(2,1)} %get-tuple-element.102.n2, f32[512,128]{1,0:T(8,128)} %get-tuple-element.103.r2, bf16[1,2,768]{2,1,0:T(2,128)(2,1)} %gains.7), custom_call_target="tpu_custom_call" | custom-call | flops 11796480 | bytes 5000000 | tf_op jit(solution)/shard_map/second_norm_backward/pallas_call | solution.py:125
  117.0 3.1 collective-permute-start.12
  120.1 13.6 %ffn_backward.2 = (bf16[512,768]{1,0:T(8,128)(2,1)}, f32[512,768]{1,0:T(8,128)}, f32[8,768]{1,0:T(8,128)}, f32[8,3072]{1,0:T(8,128)}, bf16[512,3072]{1,0:T(8,128)(2,1)}) custom-call(bf16[512,768]{1,0:T(8,128)(2,1)} %get-tuple-element.104.ddown.refs_2_, f32[512,768]{1,0:T(8,128)} %get-tuple-element.105.dsum2, bf16[512,768]{1,0:T(8,128)(2,1)} %get-tuple-element.106.n1, ...), custom_call_target="tpu_custom_call" | custom-call | flops 4831838208 | bytes 24000000 | tf_op jit(solution)/shard_map/ffn_backward/pallas_call | solution.py:125
  133.7 14.8 %attention_backward.2 = (bf16[512,768]{1,0:T(8,128)(2,1)}, f32[8,768]{1,0:T(8,128)}, bf16[512,2304]{1,0:T(8,128)(2,1)}) custom-call(bf16[512,768]{1,0:T(8,128)(2,1)} %get-tuple-element.109.datt.refs_9_, f32[512,768]{1,0:T(8,128)} %get-tuple-element.110.dsum1, bf16[512,2304]{1,0:T(8,128)(2,1)} %get-tuple-element.111.qkv_h, ...), custom_call_target="tpu_custom_call" | custom-call | flops 3422552064 | bytes 22000000 | tf_op jit(solution)/shard_map/attention_backward/pallas_call | solution.py:125
  148.6 1.3 collective-permute-start.10
  151.1 17.6 %ffn_weights.2 = (bf16[4,384,768]{2,1,0:T(8,128)(2,1)}, bf16[4,384,768]{2,1,0:T(8,128)(2,1)}) custom-call(bf16[512,768]{1,0:T(8,128)(2,1)} %get-tuple-element.114.refs_0_, bf16[512,768]{1,0:T(8,128)(2,1)} %copy-done.18, bf16[512,768]{1,0:T(8,128)(2,1)} %get-tuple-element.104.ddown.refs_2_, bf16[512,768]{1,0:T(8,128)(2,1)} %copy-done.20, ...), custom_call_target="tpu_custom_call" | custom-call | flops 7247757312 | bytes 20000000 | tf_op jit(solution)/shard_map/ffn_weights/pallas_call | solution.py:125
  168.7 0.9 copy-done.4
  169.6 3.7 %second_norm_backward.3 = (bf16[512,768]{1,0:T(8,128)(2,1)}, f32[512,768]{1,0:T(8,128)}, f32[8,768]{1,0:T(8,128)}) custom-call(s32[2]{0:T(128)} %lens.3, bf16[512,768]{1,0:T(8,128)(2,1)} %copy-done.4, bf16[512,768]{1,0:T(8,128)(2,1)} %get-tuple-element.102.n2, f32[512,128]{1,0:T(8,128)} %get-tuple-element.103.r2, bf16[1,2,768]{2,1,0:T(2,128)(2,1)} %gains.7), custom_call_target="tpu_custom_call" | custom-call | flops 11796480 | bytes 5000000 | tf_op jit(solution)/shard_map/second_norm_backward/pallas_call | solution.py:125
  174.1 9.4 %attention_weights.3 = (bf16[8,208,768]{2,1,0:T(8,128)(2,1)}, bf16[8,208,768]{2,1,0:T(8,128)(2,1)}) custom-call(bf16[2,128,768]{2,1,0:T(8,128)(2,1)} %refs_0_.9, bf16[2,128,768]{2,1,0:T(8,128)(2,1)} %copy-done.12, bf16[512,768]{1,0:T(8,128)(2,1)} %copy-done.17, f32[8,768]{1,0:T(8,128)} %get-tuple-element.136.refs_3_, f32[8,768]{1,0:T(8,128)} %get-tuple-element.137.refs_4_, ...), custom_call_target="tpu_custom_call" | custom-call | flops 2415919104 | bytes 12000000 | tf_op jit(solution)/shard_map/attention_weights/pallas_call | solution.py:125
  183.4 2.2 collective-permute-start.17
  185.6 4.2 %ffn_backward.3 = (bf16[512,768]{1,0:T(8,128)(2,1)}, f32[512,768]{1,0:T(8,128)}, f32[8,768]{1,0:T(8,128)}, f32[8,3072]{1,0:T(8,128)}, bf16[512,3072]{1,0:T(8,128)(2,1)}) custom-call(bf16[512,768]{1,0:T(8,128)(2,1)} %get-tuple-element.121.ddown.refs_2_, f32[512,768]{1,0:T(8,128)} %get-tuple-element.122.dsum2, bf16[512,768]{1,0:T(8,128)(2,1)} %get-tuple-element.106.n1, ...), custom_call_target="tpu_custom_call" | custom-call | flops 4831838208 | bytes 24000000 | tf_op jit(solution)/shard_map/ffn_backward/pallas_call | solution.py:125
  189.8 0.9 copy-done.19
  190.7 1.2 ffn_weights.3
  192.0 9.4 %attention_backward.3 = (bf16[512,768]{1,0:T(8,128)(2,1)}, f32[8,768]{1,0:T(8,128)}, bf16[512,2304]{1,0:T(8,128)(2,1)}) custom-call(bf16[512,768]{1,0:T(8,128)(2,1)} %get-tuple-element.128.datt.refs_9_, f32[512,768]{1,0:T(8,128)} %get-tuple-element.129.dsum1, bf16[512,2304]{1,0:T(8,128)(2,1)} %get-tuple-element.111.qkv_h, ...), custom_call_target="tpu_custom_call" | custom-call | flops 3422552064 | bytes 22000000 | tf_op jit(solution)/shard_map/attention_backward/pallas_call | solution.py:125
  202.0 1.9 attention_weights.2
  204.7 1.9 collective-permute-start.16
  206.7 2.1 collective-permute-start.15
  208.8 6.5 %collective-permute-done.17.refs_1_.refs_7_ = bf16[8,208,768]{2,1,0:T(8,128)(2,1)S(1)} collective-permute-done((bf16[8,208,768]{2,1,0:T(8,128)(2,1)}, bf16[8,208,768]{2,1,0:T(8,128)(2,1)S(1)}, u32[]{:S(2)}, u32[]{:S(2)}) %collective-permute-start.17) | collective-permute-done | bytes 2555936 | tf_op jit(solution)/shard_map/ppermute | solution.py:797
  215.3 1.5 copy-done
  216.8 3.4 partial_sums.6
  220.2 1.9 collective-permute-start.19
  222.1 16.2 %collective-permute-done.16.refs_1_.refs_6_ = bf16[4,384,768]{2,1,0:T(8,128)(2,1)} collective-permute-done((bf16[4,384,768]{2,1,0:T(8,128)(2,1)S(1)}, bf16[4,384,768]{2,1,0:T(8,128)(2,1)}, u32[]{:S(2)}, u32[]{:S(2)}) %collective-permute-start.16) | collective-permute-done | bytes 2359328 | tf_op jit(solution)/shard_map/ppermute | solution.py:797
  238.3 4.0 %partial_sums.7 = (bf16[384,768]{1,0:T(8,128)(2,1)}, bf16[384,768]{1,0:T(8,128)(2,1)}, bf16[384,768]{1,0:T(8,128)(2,1)}) custom-call(bf16[4,384,768]{2,1,0:T(8,128)(2,1)} %get-tuple-element.118.refs_0_.refs_5_, bf16[4,384,768]{2,1,0:T(8,128)(2,1)} %collective-permute-done.16.refs_1_.refs_6_), custom_call_target="tpu_custom_call" | custom-call | flops 1769472 | bytes 5308416 | tf_op jit(solution)/shard_map/partial_sums/pallas_call | solution.py:125
  243.3 1.5 copy-done.1
  246.4 3.9 %collective-permute-start.26 = (bf16[384,768]{1,0:T(8,128)(2,1)S(1)}, bf16[384,768]{1,0:T(8,128)(2,1)S(1)}, u32[]{:S(2)}, u32[]{:S(2)}) collective-permute-start(bf16[384,768]{1,0:T(8,128)(2,1)S(1)} %copy-done.21), channel_id=1, source_target_pairs={{16,20},{17,21},{18,22},{19,23},{20,16},{21,17},{22,18},{23,19},{2... | collective-permute-start | bytes 1769480 | tf_op jit(solution)/shard_map/ppermute | solution.py:797
  250.3 3.3 collective-permute-start.27
  253.6 1.9 collective-permute-start.28
  255.5 6.0 %collective-permute-done.26.refs_7_ = bf16[384,768]{1,0:T(8,128)(2,1)S(1)} collective-permute-done((bf16[384,768]{1,0:T(8,128)(2,1)S(1)}, bf16[384,768]{1,0:T(8,128)(2,1)S(1)}, u32[]{:S(2)}, u32[]{:S(2)}) %collective-permute-start.26) | collective-permute-done | bytes 589856 | tf_op jit(solution)/shard_map/ppermute | solution.py:797
  262.2 11.2 %collective-permute-done.27.refs_8_ = bf16[384,768]{1,0:T(8,128)(2,1)S(1)} collective-permute-done((bf16[384,768]{1,0:T(8,128)(2,1)}, bf16[384,768]{1,0:T(8,128)(2,1)S(1)}, u32[]{:S(2)}, u32[]{:S(2)}) %collective-permute-start.27) | collective-permute-done | bytes 589856 | tf_op jit(solution)/shard_map/ppermute | solution.py:797
  273.4 1.5 collective-permute-start.24
  274.9 1.5 collective-permute-start.25
  276.4 3.5 partial_sums.10
  279.9 3.3 collective-permute-start.29
  284.1 3.3 collective-permute-start.30
  287.9 3.4 collective-permute-start.31
  291.3 1.4 collective-permute-start.20
  292.7 1.4 collective-permute-start.21
  294.1 1.4 collective-permute-start.22
  295.6 4.0 %ffn_total.1 = (f32[192,768]{1,0:T(8,128)}, f32[96,768]{1,0:T(8,128)}, bf16[96,768]{1,0:T(8,128)(2,1)}) custom-call(bf16[4,384,768]{2,1,0:T(8,128)(2,1)} %get-tuple-element.127.refs_0_, bf16[4,384,768]{2,1,0:T(8,128)(2,1)} %collective-permute-done.15.refs_1_, bf16[384,768]{1,0:T(8,128)(2,1)} %copy-done.10, bf16[384,768]{1,0:T(8,128)(2,1)} %collective-permute-done.24.refs_3_, ...), custom_call_target="tpu_custom_call" | custom-call | flops 1000000 | bytes 4000000 | tf_op jit(solution)/shard_map/ffn_total/pallas_call | solution.py:125
  299.7 1.3 collective-permute-start.33
  301.0 18.6 %collective-permute-done.31.refs_11_ = bf16[208,768]{1,0:T(8,128)(2,1)} collective-permute-done((bf16[208,768]{1,0:T(8,128)(2,1)}, bf16[208,768]{1,0:T(8,128)(2,1)}, u32[]{:S(2)}, u32[]{:S(2)}) %collective-permute-start.31) | collective-permute-done | bytes 319520 | tf_op jit(solution)/shard_map/ppermute | solution.py:797
  319.5 2.3 collective-permute-start.34
  321.9 3.5 attention_total.1
  326.0 26.8 %collective-permute-start.32 = (f32[128]{0:T(128)S(1)}, f32[128]{0:T(128)S(1)}, u32[]{:S(2)}, u32[]{:S(2)}) collective-permute-start(f32[128]{0:T(128)S(1)} %slice_bitcast_fusion), channel_id=1, source_target_pairs={{16,0},{17,1},{18,2},{19,3},{20,4},{21,5},{22,6},{23,7},{24,8},{25... | collective-permute-start | bytes 1544 | tf_op jit(solution)/shard_map/ppermute | solution.py:990
  353.6 2.7 up_total.1
  356.3 1.3 copy.31
  357.6 1.2 broadcast_select_fusion.1
  358.7 0.9 fusion
  (90 shorter events, 15.9 us)
Async XLA Ops:
  0.6 11.6 %collective-permute-start.1 = (bf16[2,128,768]{2,1,0:T(8,128)(2,1)}, bf16[2,128,768]{2,1,0:T(8,128)(2,1)S(1)}, u32[]{:S(2)}, u32[]{:S(2)}) collective-permute-start(bf16[2,128,768]{2,1,0:T(8,128)(2,1)} %refs_1_.3), channel_id=1, source_target_pairs={{16,0},{17,1},{18,2},{19,3},{20,4},{21,5},{22,6},{23,7},{24,8},{25... | collective-permute-start | bytes 1179656 | tf_op jit(solution)/shard_map/ppermute | solution.py:990
  12.3 0.7 copy-start.22
  13.0 3.9 %copy-start.11 = (bf16[2,128,768]{2,1,0:T(8,128)(2,1)S(1)}, bf16[2,128,768]{2,1,0:T(8,128)(2,1)}, u32[]{:S(2)}) copy-start(bf16[2,128,768]{2,1,0:T(8,128)(2,1)} %refs_0_.9) | copy-start | bytes 1179652
  15.6 16.3 %collective-permute-start.2 = (bf16[512,768]{1,0:T(8,128)(2,1)}, bf16[512,768]{1,0:T(8,128)(2,1)S(1)}, u32[]{:S(2)}, u32[]{:S(2)}) collective-permute-start(bf16[512,768]{1,0:T(8,128)(2,1)} %get-tuple-element.94), channel_id=1, source_target_pairs={{0,16},{1,17},{2,18},{3,19},{4,20},{5,21},{6,22},{7,23},{8,24},{9,... | collective-permute-start | bytes 2359304 | tf_op jit(solution)/shard_map/ppermute | solution.py:990
  16.9 15.0 %collective-permute-start = (bf16[2,128,768]{2,1,0:T(8,128)(2,1)S(1)}, bf16[2,128,768]{2,1,0:T(8,128)(2,1)S(1)}, u32[]{:S(2)}, u32[]{:S(2)}) collective-permute-start(bf16[2,128,768]{2,1,0:T(8,128)(2,1)S(1)} %copy-done.11), channel_id=1, source_target_pairs={{16,0},{17,1},{18,2},{19,3},{20,4},{21,5},{22,6},{23,7},{24,8},{25... | collective-permute-start | bytes 1179656 | tf_op jit(solution)/shard_map/ppermute | solution.py:990
  31.9 0.7 copy-start.12
  31.9 1.0 copy-start.6
  33.0 26.1 %copy-start.15 = (s32[2]{0:T(128)S(1)}, s32[2]{0:T(128)}, u32[]{:S(2)}) copy-start(s32[2]{0:T(128)} %param.25) | copy-start | bytes 28
  54.4 7.3 %collective-permute-start.3 = (bf16[512,768]{1,0:T(8,128)(2,1)}, bf16[512,768]{1,0:T(8,128)(2,1)S(1)}, u32[]{:S(2)}, u32[]{:S(2)}) collective-permute-start(bf16[512,768]{1,0:T(8,128)(2,1)} %get-tuple-element.95), channel_id=1, source_target_pairs={{0,16},{1,17},{2,18},{3,19},{4,20},{5,21},{6,22},{7,23},{8,24},{9,... | collective-permute-start | bytes 2359304 | tf_op jit(solution)/shard_map/ppermute | solution.py:990
  56.4 3.4 collective-permute-start.6
  58.6 2.8 collective-permute-start.5
  58.9 2.8 collective-permute-start.4
  61.7 0.9 copy-start.17
  97.7 4.8 %collective-permute-start.9 = (f32[8,768]{1,0:T(8,128)S(1)}, f32[8,768]{1,0:T(8,128)S(1)}, u32[]{:S(2)}, u32[]{:S(2)}) collective-permute-start(f32[8,768]{1,0:T(8,128)S(1)} %pad_maximum_fusion.1), channel_id=1, source_target_pairs={{0,12},{1,13},{2,14},{3,15},{4,8},{5,9},{6,10},{7,11},{8,4},{9,5},... | collective-permute-start | bytes 73736 | tf_op jit(solution)/shard_map/ppermute | solution.py:797
  99.0 3.6 collective-permute-start.8
  100.1 2.8 collective-permute-start.7
  101.2 48.7 %collective-permute-start.11 = (bf16[512,768]{1,0:T(8,128)(2,1)}, bf16[512,768]{1,0:T(8,128)(2,1)S(1)}, u32[]{:S(2)}, u32[]{:S(2)}) collective-permute-start(bf16[512,768]{1,0:T(8,128)(2,1)} %get-tuple-element.114.refs_0_), channel_id=1, source_target_pairs={{0,2},{1,3},{2,0},{3,1},{4,6},{5,7},{6,4},{7,5},{8,10},{9,11},{10,... | collective-permute-start | bytes 2359304 | tf_op jit(solution)/shard_map/ppermute | solution.py:797
  117.0 32.9 %collective-permute-start.12 = (bf16[512,768]{1,0:T(8,128)(2,1)}, bf16[512,768]{1,0:T(8,128)(2,1)S(1)}, u32[]{:S(2)}, u32[]{:S(2)}) collective-permute-start(bf16[512,768]{1,0:T(8,128)(2,1)} %get-tuple-element.104.ddown.refs_2_), channel_id=1, source_target_pairs={{16,18},{17,19},{18,16},{19,17},{20,22},{21,23},{22,20},{23,21},{2... | collective-permute-start | bytes 2359304 | tf_op jit(solution)/shard_map/ppermute | solution.py:797
  148.6 20.1 %collective-permute-start.10 = (bf16[512,768]{1,0:T(8,128)(2,1)}, bf16[512,768]{1,0:T(8,128)(2,1)S(1)}, u32[]{:S(2)}, u32[]{:S(2)}) collective-permute-start(bf16[512,768]{1,0:T(8,128)(2,1)} %get-tuple-element.113), channel_id=1, source_target_pairs={{16,0},{17,1},{18,2},{19,3},{20,4},{21,5},{22,6},{23,7},{24,8},{25... | collective-permute-start | bytes 2359304 | tf_op jit(solution)/shard_map/ppermute | solution.py:990
  149.9 0.9 copy-start.18
  149.9 1.1 copy-start.20
  168.7 0.9 copy-start.4
  173.3 16.5 %collective-permute-start.13 = (bf16[512,768]{1,0:T(8,128)(2,1)}, bf16[512,768]{1,0:T(8,128)(2,1)S(1)}, u32[]{:S(2)}, u32[]{:S(2)}) collective-permute-start(bf16[512,768]{1,0:T(8,128)(2,1)} %get-tuple-element.121.ddown.refs_2_), channel_id=1, source_target_pairs={{0,2},{1,3},{2,0},{3,1},{4,6},{5,7},{6,4},{7,5},{8,10},{9,11},{10,... | collective-permute-start | bytes 2359304 | tf_op jit(solution)/shard_map/ppermute | solution.py:797
  183.4 31.9 %collective-permute-start.17 = (bf16[8,208,768]{2,1,0:T(8,128)(2,1)}, bf16[8,208,768]{2,1,0:T(8,128)(2,1)S(1)}, u32[]{:S(2)}, u32[]{:S(2)}) collective-permute-start(bf16[8,208,768]{2,1,0:T(8,128)(2,1)} %get-tuple-element.143), channel_id=1, source_target_pairs={{16,18},{17,19},{18,16},{19,17},{20,22},{21,23},{22,20},{23,21},{2... | collective-permute-start | bytes 7667720 | tf_op jit(solution)/shard_map/ppermute | solution.py:797
  189.8 0.9 copy-start.19
  202.0 2.8 copy-start.16
  203.9 39.4 %collective-permute-start.14 = (bf16[8,208,768]{2,1,0:T(8,128)(2,1)}, bf16[8,208,768]{2,1,0:T(8,128)(2,1)S(1)}, u32[]{:S(2)}, u32[]{:S(2)}) collective-permute-start(bf16[8,208,768]{2,1,0:T(8,128)(2,1)} %get-tuple-element.135), channel_id=1, source_target_pairs={{0,2},{1,3},{2,0},{3,1},{4,6},{5,7},{6,4},{7,5},{8,10},{9,11},{10,... | collective-permute-start | bytes 7667720 | tf_op jit(solution)/shard_map/ppermute | solution.py:797
  204.7 33.6 %collective-permute-start.16 = (bf16[4,384,768]{2,1,0:T(8,128)(2,1)S(1)}, bf16[4,384,768]{2,1,0:T(8,128)(2,1)}, u32[]{:S(2)}, u32[]{:S(2)}) collective-permute-start(bf16[4,384,768]{2,1,0:T(8,128)(2,1)S(1)} %copy-done.16), channel_id=1, source_target_pairs={{16,17},{17,16},{18,19},{19,18},{20,21},{21,20},{22,23},{23,22},{2... | collective-permute-start | bytes 7077896 | tf_op jit(solution)/shard_map/ppermute | solution.py:797
  206.7 35.7 %collective-permute-start.15 = (bf16[4,384,768]{2,1,0:T(8,128)(2,1)}, bf16[4,384,768]{2,1,0:T(8,128)(2,1)}, u32[]{:S(2)}, u32[]{:S(2)}) collective-permute-start(bf16[4,384,768]{2,1,0:T(8,128)(2,1)} %get-tuple-element.126), channel_id=1, source_target_pairs={{0,1},{1,0},{2,3},{3,2},{4,5},{5,4},{6,7},{7,6},{8,9},{9,8},{10,11... | collective-permute-start | bytes 7077896 | tf_op jit(solution)/shard_map/ppermute | solution.py:797
  215.3 1.5 copy-start
  220.2 54.7 %collective-permute-start.19 = (bf16[4,208,768]{2,1,0:T(8,128)(2,1)}, bf16[4,208,768]{2,1,0:T(8,128)(2,1)S(1)}, u32[]{:S(2)}, u32[]{:S(2)}) collective-permute-start(bf16[4,208,768]{2,1,0:T(8,128)(2,1)} %partial_sums.6), channel_id=1, source_target_pairs={{16,17},{17,16},{18,19},{19,18},{20,21},{21,20},{22,23},{23,22},{2... | collective-permute-start | bytes 3833864 | tf_op jit(solution)/shard_map/ppermute | solution.py:797
  243.3 1.5 copy-start.1
  244.8 1.6 copy-start.21
  245.7 34.2 %collective-permute-start.18 = (bf16[4,208,768]{2,1,0:T(8,128)(2,1)}, bf16[4,208,768]{2,1,0:T(8,128)(2,1)S(1)}, u32[]{:S(2)}, u32[]{:S(2)}) collective-permute-start(bf16[4,208,768]{2,1,0:T(8,128)(2,1)} %partial_sums.9), channel_id=1, source_target_pairs={{0,1},{1,0},{2,3},{3,2},{4,5},{5,4},{6,7},{7,6},{8,9},{9,8},{10,11... | collective-permute-start | bytes 3833864 | tf_op jit(solution)/shard_map/ppermute | solution.py:797
  246.4 15.1 %collective-permute-start.26 = (bf16[384,768]{1,0:T(8,128)(2,1)S(1)}, bf16[384,768]{1,0:T(8,128)(2,1)S(1)}, u32[]{:S(2)}, u32[]{:S(2)}) collective-permute-start(bf16[384,768]{1,0:T(8,128)(2,1)S(1)} %copy-done.21), channel_id=1, source_target_pairs={{16,20},{17,21},{18,22},{19,23},{20,16},{21,17},{22,18},{23,19},{2... | collective-permute-start | bytes 1769480 | tf_op jit(solution)/shard_map/ppermute | solution.py:797
  250.3 23.1 %collective-permute-start.27 = (bf16[384,768]{1,0:T(8,128)(2,1)}, bf16[384,768]{1,0:T(8,128)(2,1)S(1)}, u32[]{:S(2)}, u32[]{:S(2)}) collective-permute-start(bf16[384,768]{1,0:T(8,128)(2,1)} %get-tuple-element.147), channel_id=1, source_target_pairs={{16,24},{17,25},{18,26},{19,27},{20,28},{21,29},{22,30},{23,31},{2... | collective-permute-start | bytes 1769480 | tf_op jit(solution)/shard_map/ppermute | solution.py:797
  253.6 30.5 %collective-permute-start.28 = (bf16[384,768]{1,0:T(8,128)(2,1)}, bf16[384,768]{1,0:T(8,128)(2,1)S(1)}, u32[]{:S(2)}, u32[]{:S(2)}) collective-permute-start(bf16[384,768]{1,0:T(8,128)(2,1)} %get-tuple-element.148), channel_id=1, source_target_pairs={{16,28},{17,29},{18,30},{19,31},{20,24},{21,25},{22,26},{23,27},{2... | collective-permute-start | bytes 1769480 | tf_op jit(solution)/shard_map/ppermute | solution.py:797
  261.5 34.0 %copy-start.7 = (bf16[384,768]{1,0:T(8,128)(2,1)}, bf16[384,768]{1,0:T(8,128)(2,1)S(1)}, u32[]{:S(2)}) copy-start(bf16[384,768]{1,0:T(8,128)(2,1)S(1)} %collective-permute-done.26.refs_7_) | copy-start | bytes 1769476
  261.5 29.8 %collective-permute-start.23 = (bf16[384,768]{1,0:T(8,128)(2,1)}, bf16[384,768]{1,0:T(8,128)(2,1)S(1)}, u32[]{:S(2)}, u32[]{:S(2)}) collective-permute-start(bf16[384,768]{1,0:T(8,128)(2,1)} %get-tuple-element.150), channel_id=1, source_target_pairs={{0,4},{1,5},{2,6},{3,7},{4,0},{5,1},{6,2},{7,3},{8,12},{9,13},{10,... | collective-permute-start | bytes 1769480 | tf_op jit(solution)/shard_map/ppermute | solution.py:797
  273.4 22.2 %copy-start.8 = (bf16[384,768]{1,0:T(8,128)(2,1)}, bf16[384,768]{1,0:T(8,128)(2,1)S(1)}, u32[]{:S(2)}) copy-start(bf16[384,768]{1,0:T(8,128)(2,1)S(1)} %collective-permute-done.27.refs_8_) | copy-start | bytes 1769476
  273.4 19.3 %collective-permute-start.24 = (bf16[384,768]{1,0:T(8,128)(2,1)}, bf16[384,768]{1,0:T(8,128)(2,1)}, u32[]{:S(2)}, u32[]{:S(2)}) collective-permute-start(bf16[384,768]{1,0:T(8,128)(2,1)} %get-tuple-element.151), channel_id=1, source_target_pairs={{0,8},{1,9},{2,10},{3,11},{4,12},{5,13},{6,14},{7,15},{8,0},{9,1},... | collective-permute-start | bytes 1769480 | tf_op jit(solution)/shard_map/ppermute | solution.py:797
  274.9 1.5 copy-start.2
  274.9 19.3 %collective-permute-start.25 = (bf16[384,768]{1,0:T(8,128)(2,1)}, bf16[384,768]{1,0:T(8,128)(2,1)}, u32[]{:S(2)}, u32[]{:S(2)}) collective-permute-start(bf16[384,768]{1,0:T(8,128)(2,1)} %get-tuple-element.152), channel_id=1, source_target_pairs={{0,12},{1,13},{2,14},{3,15},{4,8},{5,9},{6,10},{7,11},{8,4},{9,5},... | collective-permute-start | bytes 1769480 | tf_op jit(solution)/shard_map/ppermute | solution.py:797
  279.9 3.3 copy-start.3
  279.9 7.9 %collective-permute-start.29 = (bf16[208,768]{1,0:T(8,128)(2,1)}, bf16[208,768]{1,0:T(8,128)(2,1)S(1)}, u32[]{:S(2)}, u32[]{:S(2)}) collective-permute-start(bf16[208,768]{1,0:T(8,128)(2,1)} %get-tuple-element.155), channel_id=1, source_target_pairs={{16,20},{17,21},{18,22},{19,23},{20,16},{21,17},{22,18},{23,19},{2... | collective-permute-start | bytes 958472 | tf_op jit(solution)/shard_map/ppermute | solution.py:797
  283.2 12.3 %copy-start.5 = (bf16[512,768]{1,0:T(8,128)(2,1)S(1)}, bf16[512,768]{1,0:T(8,128)(2,1)}, u32[]{:S(2)}) copy-start(bf16[512,768]{1,0:T(8,128)(2,1)} %get-tuple-element.166) | copy-start | bytes 2359300
  284.1 11.5 %copy-start.9 = (bf16[384,768]{1,0:T(8,128)(2,1)}, bf16[384,768]{1,0:T(8,128)(2,1)S(1)}, u32[]{:S(2)}) copy-start(bf16[384,768]{1,0:T(8,128)(2,1)S(1)} %collective-permute-done.28.refs_9_) | copy-start | bytes 1769476
  284.1 15.5 %collective-permute-start.30 = (bf16[208,768]{1,0:T(8,128)(2,1)}, bf16[208,768]{1,0:T(8,128)(2,1)}, u32[]{:S(2)}, u32[]{:S(2)}) collective-permute-start(bf16[208,768]{1,0:T(8,128)(2,1)} %get-tuple-element.156), channel_id=1, source_target_pairs={{16,24},{17,25},{18,26},{19,27},{20,28},{21,29},{22,30},{23,31},{2... | collective-permute-start | bytes 958472 | tf_op jit(solution)/shard_map/ppermute | solution.py:797
  287.9 3.5 copy-start.13
  287.9 31.7 %collective-permute-start.31 = (bf16[208,768]{1,0:T(8,128)(2,1)}, bf16[208,768]{1,0:T(8,128)(2,1)}, u32[]{:S(2)}, u32[]{:S(2)}) collective-permute-start(bf16[208,768]{1,0:T(8,128)(2,1)} %get-tuple-element.157), channel_id=1, source_target_pairs={{16,28},{17,29},{18,30},{19,31},{20,24},{21,25},{22,26},{23,27},{2... | collective-permute-start | bytes 958472 | tf_op jit(solution)/shard_map/ppermute | solution.py:797
  291.3 4.3 %copy-start.10 = (bf16[384,768]{1,0:T(8,128)(2,1)}, bf16[384,768]{1,0:T(8,128)(2,1)S(1)}, u32[]{:S(2)}) copy-start(bf16[384,768]{1,0:T(8,128)(2,1)S(1)} %collective-permute-done.23.refs_2_) | copy-start | bytes 1769476
  291.3 30.5 %collective-permute-start.20 = (bf16[208,768]{1,0:T(8,128)(2,1)}, bf16[208,768]{1,0:T(8,128)(2,1)}, u32[]{:S(2)}, u32[]{:S(2)}) collective-permute-start(bf16[208,768]{1,0:T(8,128)(2,1)} %get-tuple-element.159), channel_id=1, source_target_pairs={{0,4},{1,5},{2,6},{3,7},{4,0},{5,1},{6,2},{7,3},{8,12},{9,13},{10,... | collective-permute-start | bytes 958472 | tf_op jit(solution)/shard_map/ppermute | solution.py:797
  292.7 29.2 %collective-permute-start.21 = (bf16[208,768]{1,0:T(8,128)(2,1)}, bf16[208,768]{1,0:T(8,128)(2,1)}, u32[]{:S(2)}, u32[]{:S(2)}) collective-permute-start(bf16[208,768]{1,0:T(8,128)(2,1)} %get-tuple-element.160), channel_id=1, source_target_pairs={{0,8},{1,9},{2,10},{3,11},{4,12},{5,13},{6,14},{7,15},{8,0},{9,1},... | collective-permute-start | bytes 958472 | tf_op jit(solution)/shard_map/ppermute | solution.py:797
  294.1 27.7 %collective-permute-start.22 = (bf16[208,768]{1,0:T(8,128)(2,1)}, bf16[208,768]{1,0:T(8,128)(2,1)}, u32[]{:S(2)}, u32[]{:S(2)}) collective-permute-start(bf16[208,768]{1,0:T(8,128)(2,1)} %get-tuple-element.161), channel_id=1, source_target_pairs={{0,12},{1,13},{2,14},{3,15},{4,8},{5,9},{6,10},{7,11},{8,4},{9,5},... | collective-permute-start | bytes 958472 | tf_op jit(solution)/shard_map/ppermute | solution.py:797
  299.7 59.1 %collective-permute-start.33 = (bf16[2,128,768]{2,1,0:T(8,128)(2,1)S(1)}, bf16[2,128,768]{2,1,0:T(8,128)(2,1)S(1)}, u32[]{:S(2)}, u32[]{:S(2)}) collective-permute-start(bf16[2,128,768]{2,1,0:T(8,128)(2,1)S(1)} %slice.23), channel_id=1, source_target_pairs={{0,16},{1,17},{2,18},{3,19},{4,20},{5,21},{6,22},{7,23},{8,24},{9,... | collective-permute-start | bytes 1179656 | tf_op jit(solution)/shard_map/ppermute | solution.py:990
  319.5 33.4 %collective-permute-start.34 = (bf16[96,768]{1,0:T(8,128)(2,1)}, bf16[96,768]{1,0:T(8,128)(2,1)S(1)}, u32[]{:S(2)}, u32[]{:S(2)}) collective-permute-start(bf16[96,768]{1,0:T(8,128)(2,1)} %get-tuple-element.171), channel_id=1, source_target_pairs={{0,2},{1,3},{2,0},{3,1},{4,6},{5,7},{6,4},{7,5},{8,10},{9,11},{10,... | collective-permute-start | bytes 442376 | tf_op jit(solution)/shard_map/ppermute | solution.py:797
  326.0 31.5 %collective-permute-start.32 = (f32[128]{0:T(128)S(1)}, f32[128]{0:T(128)S(1)}, u32[]{:S(2)}, u32[]{:S(2)}) collective-permute-start(f32[128]{0:T(128)S(1)} %slice_bitcast_fusion), channel_id=1, source_target_pairs={{16,0},{17,1},{18,2},{19,3},{20,4},{21,5},{22,6},{23,7},{24,8},{25... | collective-permute-start | bytes 1544 | tf_op jit(solution)/shard_map/ppermute | solution.py:990
  352.9 0.7 copy-start.14
